TPU v7x, 256 devices: a whole 4x4x8 slice. The times are simulated.
256 devices in a mesh: gx: 16 (over y, x), gy: 16 (over z, core).
Axes of the slice: x: 4, y: 4, z: 8, core: 2. Of those that a mesh axis runs over, the one named last changes fastest.
Arguments:
- field: float32 [4, 768, 768, 32], P(None, 'gx', 'gy'), may hold values from -6 to 6
- w_coarse: float32 [32, 32], replicated, may hold values from -1 to 1
- w_detail: float32 [32, 32], replicated, may hold values from -1 to 1
- w_skip: float32 [32, 32], replicated, may hold values from -1 to 1
- cotangent: float32 [4, 768, 768, 32], P(None, 'gx', 'gy'), may hold values from -6 to 6
Outputs:
- grad_field: float32 [4, 768, 768, 32], P(None, 'gx', 'gy')
- grad_coarse: float32 [32, 32], replicated
- grad_detail: float32 [32, 32], replicated
- grad_skip: float32 [32, 32], replicated
All inputs are finite; a program needn't handle non-finite values.
Results may differ from a plain program's by a relative error of at most 0.00005.
Values sent between devices are 32-bit elements; how exact they have to be, the bound alone decides.
A program may use at most 128 MiB of HBM per device.

v0:
```python
import functools

import jax
import jax.numpy as jnp
import numpy as np
from jax import lax
from jax.experimental import pallas as pl
from jax.experimental.pallas import tpu as pltpu
from jax.sharding import PartitionSpec as P

LOW_TAPS = [
    0.23037781330885523,
    0.7148465705525415,
    0.6308807679295904,
    -0.02798376941698385,
    -0.18703481171888114,
    0.030841381835986965,
    0.032883011666982945,
    -0.010597401784997278,
]
HIGH_TAPS = [(-1) ** offset * LOW_TAPS[7 - offset] for offset in range(8)]

F32 = jnp.float32
BF16 = jnp.bfloat16
MESH = pl.DeviceIdType.MESH
CH = 32
BATCH = 4
CELLS = 48
COARSE = 6
ROWS = COARSE * CH
GELU_A = 0.7978845608028654
GELU_B = GELU_A * 0.044715


def bounds(low, high):
    return -((7 - low) // 2), high // 2


LEVELS = [(0, CELLS - 1)]
for _ in range(3):
    LEVELS.append(bounds(*LEVELS[-1]))


def line_matrix():
    values = np.eye(CELLS)
    low, high = LEVELS[0]
    outputs = []
    for level in range(3):
        bank = [LOW_TAPS] if level < 2 else [LOW_TAPS, HIGH_TAPS]
        first, last = LEVELS[level + 1]
        outputs = []
        for taps in bank:
            result = np.zeros((last - first + 1, CELLS))
            for k in range(first, last + 1):
                for j in range(8):
                    if low <= 2 * k + j <= high:
                        result[k - first] += taps[j] * values[2 * k + j - low]
            outputs.append(result)
        values, low, high = outputs[0], first, last
    return np.stack(outputs)


def bank_matrix():
    line = line_matrix()
    result = np.zeros((2, BATCH, 64, 2, 2, 2, 32))
    for xband in range(2):
        for b in range(BATCH):
            for part in range(2):
                for yband in range(2):
                    for k in range(COARSE):
                        result[xband, b, :CELLS, part, xband, yband, k * BATCH + b] = line[yband, part * COARSE + k]
    return result.reshape(512, 256).astype(np.float32)


def split(values):
    high = values.astype(BF16)
    return high, (values - high.astype(F32)).astype(BF16)


def dot3(left, right, dims=((1,), (0,))):
    form = (dims, ((), ()))
    total = lax.dot_general(left[0], right[0], form, preferred_element_type=F32)
    total += lax.dot_general(left[1], right[0], form, preferred_element_type=F32)
    return total + lax.dot_general(left[0], right[1], form, preferred_element_type=F32)


NT = ((1,), (1,))


class Analysis:
    def __init__(self, load):
        self.load = load
        self.memo = {}

    def get(self, level, k, taps=LOW_TAPS, band=0):
        if level == 0:
            if (0, k) not in self.memo:
                self.memo[0, k] = self.load(k)
            return self.memo[0, k]
        key = (level, k, band)
        if key not in self.memo:
            low, high = LEVELS[level - 1]
            total = None
            for j in range(8):
                if low <= 2 * k + j <= high:
                    term = self.get(level - 1, 2 * k + j) * F32(taps[j])
                    total = term if total is None else total + term
            self.memo[key] = total
        return self.memo[key]


class Synthesis:
    def __init__(self, load):
        self.load = load
        self.memo = {}

    def top(self, band, k):
        if (band, k) not in self.memo:
            self.memo[band, k] = self.load(band, k)
        return self.memo[band, k]

    def get(self, level, i):
        key = (level, i, "s")
        if key not in self.memo:
            low, high = LEVELS[level + 1]
            total = None
            for k in range(low, high + 1):
                j = i - 2 * k
                if 0 <= j < 8:
                    if level == 2:
                        term = self.top(0, k) * F32(LOW_TAPS[j]) + self.top(1, k) * F32(HIGH_TAPS[j])
                    else:
                        term = self.get(level + 1, k) * F32(LOW_TAPS[j])
                    total = term if total is None else total + term
            self.memo[key] = total
        return self.memo[key]


def kernel(
    nx, ny, field_hbm, cot_hbm, wc_ref, wd_ref, ws_ref, bh_ref, bl_ref,
    out_hbm, gc_ref, gd_ref, gs_ref,
    raw, raw_cot, field, cot, grad, mixed_skip, lines, kron, out,
    send_fwd, send_mix, recv, coeffs, wide, ar_out, ar_in, ar_part, gsum,
    in_sems, out_sems, ex_send, ex_recv, ar_send, ar_recv,
):
    gx = lax.axis_index("gx")
    gy = lax.axis_index("gy")
    right, left = lax.rem(gx + 1, nx), lax.rem(gx + nx - 1, nx)
    up, down = lax.rem(gy + 1, ny), lax.rem(gy + ny - 1, ny)

    loads = []
    for half in range(2):
        part = pl.ds(2 * half, 2)
        loads.append(pltpu.make_async_copy(field_hbm.at[part], raw.at[part], in_sems.at[half]))
    loads.append(pltpu.make_async_copy(cot_hbm, raw_cot, in_sems.at[2]))
    for load in loads:
        load.start()

    barrier = pltpu.get_barrier_semaphore()

    def greet_y(r, carry):
        pl.semaphore_signal(barrier, inc=1, device_id=(gx, lax.rem(gy + r, ny)), device_id_type=MESH)
        return carry

    def greet_x(r, carry):
        pl.semaphore_signal(barrier, inc=1, device_id=(lax.rem(gx + r, nx), gy), device_id_type=MESH)
        return carry

    lax.fori_loop(1, nx, greet_x, 0)
    lax.fori_loop(1, ny, greet_y, 0)
    pl.semaphore_signal(barrier, inc=1, device_id=(right, up), device_id_type=MESH)
    pl.semaphore_signal(barrier, inc=1, device_id=(left, down), device_id_type=MESH)

    bank = (bh_ref[...], bl_ref[...])

    def pack(source, target, half):
        columns = 128 * half
        target[:, columns : columns + 128] = jnp.zeros((CELLS * CH, 128), F32)
        for pair in range(2):
            values = source[2 * half + pair].reshape(CELLS * CH, CELLS)
            start = columns + 64 * pair
            target[:, start : start + CELLS] = values

    def column(index):
        rows = pl.multiple_of(lax.rem(index, 4) * 8, 8)
        lanes = pl.multiple_of(lax.div(index, 4) * 128, 128)
        return rows, lanes

    def analyze_column(load, rows, lanes):
        walk = Analysis(load)
        for k in range(2 * COARSE):
            for band, taps in enumerate((LOW_TAPS, HIGH_TAPS)):
                value = walk.get(3, k - COARSE, taps, band)
                lines[pl.ds(pl.multiple_of(k * CH + rows, 8), 8), pl.ds(pl.multiple_of(band * 256 + lanes, 128), 128)] = value

    def synthesis_column(rows, lanes):
        def load(band, k):
            return lines[
                pl.ds(pl.multiple_of((k + COARSE) * CH + rows, 8), 8),
                pl.ds(pl.multiple_of(band * 256 + lanes, 128), 128),
            ]

        return Synthesis(load)

    def exchange(step, sources, devices):
        copies = []
        for slot, (source, device) in enumerate(zip(sources, devices)):
            copy = pltpu.make_async_remote_copy(
                src_ref=source,
                dst_ref=recv.at[step, slot],
                send_sem=ex_send.at[step, slot],
                recv_sem=ex_recv.at[step, slot],
                device_id=device,
                device_id_type=MESH,
            )
            copy.start()
            copies.append(copy)
        return copies

    back_devices = [(left, gy), (gx, down), (left, down)]
    next_devices = [(right, gy), (gx, up), (right, up)]

    def send_partials(step):
        parts = dot3(split(lines[...]), bank)
        send_fwd[step // 2, 0] = parts[:ROWS, 128:]
        send_fwd[step // 2, 1] = parts[ROWS:, :128]
        send_fwd[step // 2, 2] = parts[:ROWS, :128]
        return parts[ROWS:, 128:], exchange(step, [send_fwd.at[step // 2, s] for s in range(3)], back_devices)

    def gather_sum(step, own, copies):
        total = own
        for slot, copy in enumerate(copies):
            copy.wait_recv()
            total = total + recv[step, slot]
        return total

    def side_by_side(values):
        return jnp.concatenate([values[k * CH : (k + 1) * CH] for k in range(COARSE)], axis=1)

    coarse_lanes = lax.broadcasted_iota(jnp.int32, (CH, 128), 1) < 32

    def mix(values, weights):
        both = dot3(weights, split(side_by_side(values)))
        chosen = [
            jnp.where(coarse_lanes, both[:CH, k * 128 : (k + 1) * 128], both[CH:, k * 128 : (k + 1) * 128])
            for k in range(COARSE)
        ]
        return jnp.concatenate(chosen, axis=0)

    def send_mixed(step, values):
        send_mix[step // 2] = values
        return exchange(step, [send_mix.at[step // 2]] * 3, next_devices)

    def synthesize_lines(step, copies):
        for copy in copies:
            copy.wait_recv()
        wide[:ROWS, :128] = recv[step, 2]
        wide[:ROWS, 128:] = recv[step, 0]
        wide[ROWS:, :128] = recv[step, 1]
        wide[ROWS:, 128:] = send_mix[step // 2]
        lines[...] = dot3(split(wide[...]), bank, NT)

    for half in range(2):
        loads[half].wait()
        pack(raw, field, half)

    def first_column(index, carry):
        rows, lanes = column(index)
        analyze_column(
            lambda x: field[pl.ds(pl.multiple_of(x * CH + rows, 8), 8), pl.ds(lanes, 128)], rows, lanes
        )
        return carry

    lax.fori_loop(0, 8, first_column, 0)
    pl.semaphore_wait(barrier, nx + ny)
    own, copies1 = send_partials(0)

    eye = (
        lax.broadcasted_iota(jnp.int32, (CH, CH), 0) == lax.broadcasted_iota(jnp.int32, (CH, CH), 1)
    ).astype(BF16)

    def transposed(weight):
        form = (NT, ((), ()))
        return lax.dot_general(eye, weight, form, preferred_element_type=F32).astype(BF16)

    coarse_parts = split(wc_ref[...])
    detail_parts = split(wd_ref[...])
    skip_parts = split(ws_ref[...])
    weights_forward = tuple(
        jnp.concatenate([transposed(c), transposed(d)], axis=0) for c, d in zip(coarse_parts, detail_parts)
    )
    weights_back = tuple(jnp.concatenate([c, d], axis=0) for c, d in zip(coarse_parts, detail_parts))

    kron[...] = jnp.zeros((4, 256, 256), F32)
    for which in range(2):
        forward = transposed(skip_parts[which]).astype(F32)
        backward = skip_parts[which].astype(F32)
        for i in range(8):
            block = slice(i * CH, (i + 1) * CH)
            kron[which, block, block] = forward
            kron[2 + which, block, block] = backward

    def skip_mix(source, first):
        weights = (kron[first].astype(BF16), kron[first + 1].astype(BF16))
        for g in range(6):
            block = slice(256 * g, 256 * g + 256)
            mixed_skip[block] = dot3(weights, split(source[block]))

    loads[2].wait()
    for half in range(2):
        pack(raw_cot, cot, half)

    coeffs[...] = gather_sum(0, own, copies1)
    copies2 = send_mixed(1, mix(coeffs[...], weights_forward))

    skip_mix(field, 0)

    synthesize_lines(1, copies2)

    def middle_column(index, carry):
        rows, lanes = column(index)
        walk = synthesis_column(rows, lanes)
        cells = pl.ds(lanes, 128)

        def load(x):
            here = pl.ds(pl.multiple_of(x * CH + rows, 8), 8)
            pre = walk.get(0, x) + mixed_skip[here, cells]
            cube = F32(GELU_B) * (pre * pre)
            tanh = jnp.tanh(pre * (F32(GELU_A) + cube))
            slope = pre * (F32(GELU_A) + F32(3.0) * cube)
            rise = (F32(0.5) + F32(0.5) * tanh) * (F32(1.0) + (slope - slope * tanh))
            value = cot[here, cells] * rise
            grad[here, cells] = value
            return value

        analyze_column(load, rows, lanes)
        return carry

    lax.fori_loop(0, 8, middle_column, 0)
    own, copies3 = send_partials(2)

    pair = jnp.zeros((256, 256), F32)
    for g in range(6):
        block = slice(256 * g, 256 * g + 256)
        pair = pair + dot3(split(field[block]), split(grad[block]), NT)
    skip_sum = pair[:CH, :CH]
    for i in range(1, 8):
        block = slice(i * CH, (i + 1) * CH)
        skip_sum = skip_sum + pair[block, block]
    skip_mix(grad, 2)

    back = gather_sum(2, own, copies3)
    copies4 = send_mixed(3, mix(back, weights_back))

    flat = side_by_side(back)
    lane = lax.rem(lax.broadcasted_iota(jnp.int32, (CH, COARSE * 128), 1), 128)
    masked = jnp.concatenate([jnp.where(lane < 32, flat, 0.0), jnp.where(lane < 32, 0.0, flat)], axis=0)
    gsum[...] = jnp.zeros((CH, 128), F32)
    gsum[:, :64] = dot3(split(side_by_side(coeffs[...])), split(masked), NT)
    gsum[:, 64:96] = skip_sum
    chunk = CH // ny
    for i in range(ny):
        ar_out[i, :chunk] = gsum[i * chunk : (i + 1) * chunk]

    def ar_copy(phase, r, source, along_x):
        size, me = (nx, gx) if along_x else (ny, gy)
        other = lax.rem(me + r, size)
        device = (other, gy) if along_x else (gx, other)
        return pltpu.make_async_remote_copy(
            src_ref=source(other),
            dst_ref=ar_in.at[phase, me],
            send_sem=ar_send.at[phase, r],
            recv_sem=ar_recv.at[phase, me],
            device_id=device,
            device_id_type=MESH,
        )

    def ar_start(phase, source, along_x):
        def step(r, carry):
            ar_copy(phase, r, source, along_x).start()
            return carry

        lax.fori_loop(1, nx if along_x else ny, step, 0)

    def ar_wait(phase, source, along_x):
        size, me = (nx, gx) if along_x else (ny, gy)

        def step(r, carry):
            other = lax.rem(me + r, size)
            arrived = ar_in.at[phase, other]
            pltpu.make_async_copy(arrived, arrived, ar_recv.at[phase, other]).wait()
            return carry

        lax.fori_loop(1, size, step, 0)

    def ar_wait_send(phase, source, along_x):
        def step(r, carry):
            ar_copy(phase, r, source, along_x).wait_send()
            return carry

        lax.fori_loop(1, nx if along_x else ny, step, 0)

    def ar_sum(phase, count):
        total = ar_in[phase, 0]
        for i in range(1, count):
            total = total + ar_in[phase, i]
        return total

    source0 = lambda other: ar_out.at[other]
    source1 = lambda other: ar_part.at[0]
    source2 = lambda other: ar_part.at[1]
    ar_in[0, gy] = ar_out[gy]
    ar_start(0, source0, False)

    ar_wait(0, source0, False)
    total = ar_sum(0, ny)
    ar_part[0] = total
    ar_in[1, gx] = total
    ar_start(1, source1, True)

    synthesize_lines(3, copies4)

    ar_wait(1, source1, True)
    total = ar_sum(1, nx)
    ar_part[1] = total
    ar_in[2, gy] = total
    ar_start(2, source2, False)

    stores = []
    for half in range(2):

        def last_column(index, carry):
            rows = pl.multiple_of(index * 8, 8)
            walk = synthesis_column(rows, 128 * half)
            for x in range(CELLS):
                here = pl.ds(pl.multiple_of(x * CH + rows, 8), 8)
                value = walk.get(0, x) + mixed_skip[here, 128 * half : 128 * half + 128]
                out[2 * half, x, pl.ds(rows, 8), :] = value[:, :CELLS]
                out[2 * half + 1, x, pl.ds(rows, 8), :] = value[:, 64 : 64 + CELLS]
            return carry

        lax.fori_loop(0, 4, last_column, 0)
        part = pl.ds(2 * half, 2)
        store = pltpu.make_async_copy(out.at[part], out_hbm.at[part], out_sems.at[half])
        store.start()
        stores.append(store)

    ar_wait(2, source2, False)
    scale = F32(1.0 / (BATCH * CELLS * CELLS * nx * ny))
    for i in range(ny):
        rows = slice(i * chunk, (i + 1) * chunk)
        values = ar_in[2, i, :chunk] * scale
        gc_ref[rows, :] = values[:, :32]
        gd_ref[rows, :] = values[:, 32:64]
        gs_ref[rows, :] = values[:, 64:96]

    for copies in (copies1, copies2, copies3, copies4):
        for copy in copies:
            copy.wait_send()
    ar_wait_send(0, source0, False)
    ar_wait_send(1, source1, True)
    ar_wait_send(2, source2, False)
    for store in stores:
        store.wait()


def shards(nx, ny, field, w_coarse, w_detail, w_skip, cotangent):
    bank = bank_matrix()
    bank_high = bank.astype(jnp.bfloat16)
    bank_low = (bank - bank_high.astype(np.float32)).astype(jnp.bfloat16)
    block = (BATCH, CELLS, CH, CELLS)
    cells = CELLS * CH
    vmem = pl.BlockSpec(memory_space=pltpu.VMEM)
    hbm = pl.BlockSpec(memory_space=pl.ANY)
    small = jax.ShapeDtypeStruct((CH, CH), F32)
    peers = max(nx, ny)


    result = pl.pallas_call(
        functools.partial(kernel, nx, ny),
        out_shape=(jax.ShapeDtypeStruct(block, F32), small, small, small),
        in_specs=[hbm, hbm, vmem, vmem, vmem, vmem, vmem],
        out_specs=(hbm, vmem, vmem, vmem),
        scratch_shapes=[
            pltpu.VMEM(block, F32),
            pltpu.VMEM(block, F32),
            pltpu.VMEM((cells, 256), F32),
            pltpu.VMEM((cells, 256), F32),
            pltpu.VMEM((cells, 256), F32),
            pltpu.VMEM((cells, 256), F32),
            pltpu.VMEM((2 * ROWS, 512), F32),
            pltpu.VMEM((4, 256, 256), F32),
            pltpu.VMEM(block, F32),
            pltpu.VMEM((2, 3, ROWS, 128), F32),
            pltpu.VMEM((2, ROWS, 128), F32),
            pltpu.VMEM((4, 3, ROWS, 128), F32),
            pltpu.VMEM((ROWS, 128), F32),
            pltpu.VMEM((2 * ROWS, 256), F32),
            pltpu.VMEM((ny, 8, 128), F32),
            pltpu.VMEM((3, peers, 8, 128), F32),
            pltpu.VMEM((2, 8, 128), F32),
            pltpu.VMEM((CH, 128), F32),
            pltpu.SemaphoreType.DMA((3,)),
            pltpu.SemaphoreType.DMA((2,)),
            pltpu.SemaphoreType.DMA((4, 3)),
            pltpu.SemaphoreType.DMA((4, 3)),
            pltpu.SemaphoreType.DMA((3, peers)),
            pltpu.SemaphoreType.DMA((3, peers)),
        ],
        compiler_params=pltpu.CompilerParams(
            collective_id=0, has_side_effects=True, vmem_limit_bytes=48 * 1024 * 1024
        ),
    )(
        jnp.transpose(field, (0, 1, 3, 2)),
        jnp.transpose(cotangent, (0, 1, 3, 2)),
        w_coarse,
        w_detail,
        w_skip,
        jnp.asarray(bank_high),
        jnp.asarray(bank_low),
    )
    return (jnp.transpose(result[0], (0, 1, 3, 2)),) + tuple(result[1:])


def solution(mesh):
    nx, ny = mesh.shape["gx"], mesh.shape["gy"]
    in_specs = (P(None, "gx", "gy", None), P(), P(), P(), P(None, "gx", "gy", None))
    out_specs = (P(None, "gx", "gy", None), P(), P(), P())

    def run(*args):
        return shards(nx, ny, *args)

    return jax.shard_map(run, mesh=mesh, in_specs=in_specs, out_specs=out_specs, check_vma=False)
```

profile of v0, /device:TPU:1, one launch (start us, length us, event | category | flops | bytes accessed | tf_op | source)
XLA Modules:
  0.0 63.0 jit_solution(8768545721516344777)
XLA Ops:
  0.6 0.0 copy-start
  0.6 0.9 %copy-done = bf16[512,256]{1,0:T(8,128)(2,1)S(1)} copy-done((bf16[512,256]{1,0:T(8,128)(2,1)S(1)}, bf16[512,256]{1,0:T(8,128)(2,1)}, u32[]{:S(2)}) %copy-start) | copy-done | bytes 262168
  1.6 0.0 copy-start.1
  1.6 0.9 %copy-done.1 = bf16[512,256]{1,0:T(8,128)(2,1)S(1)} copy-done((bf16[512,256]{1,0:T(8,128)(2,1)S(1)}, bf16[512,256]{1,0:T(8,128)(2,1)}, u32[]{:S(2)}) %copy-start.1) | copy-done | bytes 262168
  2.5 0.0 copy-start.2
  2.5 0.7 %copy-done.2 = f32[32,32]{1,0:T(8,128)S(1)} copy-done((f32[32,32]{1,0:T(8,128)S(1)}, f32[32,32]{1,0:T(8,128)}, u32[]{:S(2)}) %copy-start.2) | copy-done | bytes 4120
  3.3 0.0 copy-start.3
  3.3 0.7 %copy-done.3 = f32[32,32]{1,0:T(8,128)S(1)} copy-done((f32[32,32]{1,0:T(8,128)S(1)}, f32[32,32]{1,0:T(8,128)}, u32[]{:S(2)}) %copy-start.3) | copy-done | bytes 4120
  4.0 0.0 copy-start.4
  4.0 0.7 %copy-done.4 = f32[32,32]{1,0:T(8,128)S(1)} copy-done((f32[32,32]{1,0:T(8,128)S(1)}, f32[32,32]{1,0:T(8,128)}, u32[]{:S(2)}) %copy-start.4) | copy-done | bytes 4120
  4.7 54.8 %shard_map.102 = (f32[4,48,32,48]{3,2,1,0:T(8,128)S(1)}, f32[32,32]{1,0:T(8,128)S(1)}, f32[32,32]{1,0:T(8,128)S(1)}, f32[32,32]{1,0:T(8,128)S(1)}) custom-call(f32[4,48,32,48]{3,2,1,0:T(8,128)} %bitcast.4, f32[4,48,32,48]{3,2,1,0:T(8,128)} %bitcast.5, f32[32,32]{1,0:T(8,128)S(1)} %copy-done.2, f32[32,32]{1,0:T(8,128)S(1)} %copy-done.3, ...), custom_call_target="tpu_custom_call" | custom-call | tf_op jit(solution)/shard_map/pallas_call | solution.py:479
  59.5 1.7 %copy.15 = f32[4,48,48,32]{2,3,1,0:T(8,128)} copy(f32[4,48,48,32]{2,3,1,0:T(8,128)S(1)} %bitcast.3) | data formatting | bytes 2359296
  61.2 0.6 copy.16
  61.8 0.6 copy.17
  62.4 0.6 copy.18
Async XLA Ops:
  0.6 1.0 %copy-start = (bf16[512,256]{1,0:T(8,128)(2,1)S(1)}, bf16[512,256]{1,0:T(8,128)(2,1)}, u32[]{:S(2)}) copy-start(bf16[512,256]{1,0:T(8,128)(2,1)} %constant.5.clone.bl_ref) | copy-start | bytes 786436
  1.6 0.9 %copy-start.1 = (bf16[512,256]{1,0:T(8,128)(2,1)S(1)}, bf16[512,256]{1,0:T(8,128)(2,1)}, u32[]{:S(2)}) copy-start(bf16[512,256]{1,0:T(8,128)(2,1)} %constant.4.clone.bh_ref) | copy-start | bytes 786436
  2.5 0.7 %copy-start.2 = (f32[32,32]{1,0:T(8,128)S(1)}, f32[32,32]{1,0:T(8,128)}, u32[]{:S(2)}) copy-start(f32[32,32]{1,0:T(8,128)} %wc_ref.1) | copy-start | bytes 12292
  3.3 0.7 %copy-start.3 = (f32[32,32]{1,0:T(8,128)S(1)}, f32[32,32]{1,0:T(8,128)}, u32[]{:S(2)}) copy-start(f32[32,32]{1,0:T(8,128)} %wd_ref.1) | copy-start | bytes 12292
  4.0 0.7 %copy-start.4 = (f32[32,32]{1,0:T(8,128)S(1)}, f32[32,32]{1,0:T(8,128)}, u32[]{:S(2)}) copy-start(f32[32,32]{1,0:T(8,128)} %ws_ref.1) | copy-start | bytes 12292
where the time goes:
time: 63.4 us; the launch traced here: 63 us
  Pallas kernels  54.8 us (86%)
  local copies, waits for them, and re-layouts  7.53 us (12%)
  between operations  0.65 us (1%)
    pallas_call x1, Pallas kernels, shards(): pl.pallas_call(functools.partial(kernel, nx, ny), out_shape=(jax.ShapeDty...  54.8 us
    unnamed x14, local copies, waits for them, and re-layouts  7.53 us

commit v1 on v0

--- a/solution.py
+++ b/solution.py
@@ -136,11 +136,65 @@
         return self.memo[key]
 
 
+def column_at(index):
+    rows = pl.multiple_of(lax.rem(index, 4) * 8, 8)
+    lanes = pl.multiple_of(lax.div(index, 4) * 128, 128)
+    return rows, lanes
+
+
+def synthesis_column(lines, rows, lanes):
+    def load(band, k):
+        return lines[
+            pl.ds(pl.multiple_of((k + COARSE) * CH + rows, 8), 8),
+            pl.ds(pl.multiple_of(band * 256 + lanes, 128), 128),
+        ]
+
+    return Synthesis(load)
+
+
+def last_kernel(
+    lines_hbm, base_hbm, sum_hbm, out_hbm, gc_ref, gd_ref, gs_ref, lines, base, summed, out, in_sems, out_sems
+):
+    loads = [pltpu.make_async_copy(lines_hbm, lines, in_sems.at[0])]
+    for half in range(2):
+        lanes = pl.ds(128 * half, 128)
+        loads.append(pltpu.make_async_copy(base_hbm.at[:, lanes], base.at[:, lanes], in_sems.at[1 + half]))
+    loads.append(pltpu.make_async_copy(sum_hbm, summed, in_sems.at[3]))
+    for load in loads:
+        load.start()
+    loads[0].wait()
+    stores = []
+    for half in range(2):
+        loads[1 + half].wait()
+
+        def last_column(index, carry):
+            rows = pl.multiple_of(index * 8, 8)
+            walk = synthesis_column(lines, rows, 128 * half)
+            for x in range(CELLS):
+                here = pl.ds(pl.multiple_of(x * CH + rows, 8), 8)
+                value = walk.get(0, x) + base[here, 128 * half : 128 * half + 128]
+                out[2 * half, x, pl.ds(rows, 8), :] = value[:, :CELLS]
+                out[2 * half + 1, x, pl.ds(rows, 8), :] = value[:, 64 : 64 + CELLS]
+            return carry
+
+        lax.fori_loop(0, 4, last_column, 0)
+        part = pl.ds(2 * half, 2)
+        store = pltpu.make_async_copy(out.at[part], out_hbm.at[part], out_sems.at[half])
+        store.start()
+        stores.append(store)
+    loads[3].wait()
+    gc_ref[...] = summed[:, :32]
+    gd_ref[...] = summed[:, 32:64]
+    gs_ref[...] = summed[:, 64:96]
+    for store in stores:
+        store.wait()
+
+
 def kernel(
-    nx, ny, field_hbm, cot_hbm, wc_ref, wd_ref, ws_ref, bh_ref, bl_ref,
-    out_hbm, gc_ref, gd_ref, gs_ref,
-    raw, raw_cot, field, cot, grad, mixed_skip, lines, kron, out,
-    send_fwd, send_mix, recv, coeffs, wide, ar_out, ar_in, ar_part, gsum,
+    nx, ny, field_hbm, cot_hbm, wc_hbm, wd_hbm, ws_hbm, bank_hbm,
+    lines_hbm, base_hbm, sum_hbm,
+    raw, raw_cot, field, cot, grad, mixed_skip, lines, kron, wc_ref, wd_ref, ws_ref, bank_ref, bank_parts,
+    send_fwd, send_mix, recv, wide, ar_out, ar_in, ar_part, gsum,
     in_sems, out_sems, ex_send, ex_recv, ar_send, ar_recv,
 ):
     gx = lax.axis_index("gx")
@@ -152,7 +206,9 @@
     for half in range(2):
         part = pl.ds(2 * half, 2)
         loads.append(pltpu.make_async_copy(field_hbm.at[part], raw.at[part], in_sems.at[half]))
-    loads.append(pltpu.make_async_copy(cot_hbm, raw_cot, in_sems.at[2]))
+    small = [(bank_hbm, bank_ref), (wc_hbm, wc_ref), (wd_hbm, wd_ref), (ws_hbm, ws_ref)]
+    for slot, (source, target) in enumerate(small + [(cot_hbm, raw_cot)]):
+        loads.append(pltpu.make_async_copy(source, target, in_sems.at[2 + slot]))
     for load in loads:
         load.start()
 
@@ -170,8 +226,6 @@
     lax.fori_loop(1, ny, greet_y, 0)
     pl.semaphore_signal(barrier, inc=1, device_id=(right, up), device_id_type=MESH)
     pl.semaphore_signal(barrier, inc=1, device_id=(left, down), device_id_type=MESH)
-
-    bank = (bh_ref[...], bl_ref[...])
 
     def pack(source, target, half):
         columns = 128 * half
@@ -181,26 +235,12 @@
             start = columns + 64 * pair
             target[:, start : start + CELLS] = values
 
-    def column(index):
-        rows = pl.multiple_of(lax.rem(index, 4) * 8, 8)
-        lanes = pl.multiple_of(lax.div(index, 4) * 128, 128)
-        return rows, lanes
-
     def analyze_column(load, rows, lanes):
         walk = Analysis(load)
         for k in range(2 * COARSE):
             for band, taps in enumerate((LOW_TAPS, HIGH_TAPS)):
                 value = walk.get(3, k - COARSE, taps, band)
                 lines[pl.ds(pl.multiple_of(k * CH + rows, 8), 8), pl.ds(pl.multiple_of(band * 256 + lanes, 128), 128)] = value
-
-    def synthesis_column(rows, lanes):
-        def load(band, k):
-            return lines[
-                pl.ds(pl.multiple_of((k + COARSE) * CH + rows, 8), 8),
-                pl.ds(pl.multiple_of(band * 256 + lanes, 128), 128),
-            ]
-
-        return Synthesis(load)
 
     def exchange(step, sources, devices):
         copies = []
@@ -221,51 +261,49 @@
     next_devices = [(right, gy), (gx, up), (right, up)]
 
     def send_partials(step):
-        parts = dot3(split(lines[...]), bank)
+        parts = dot3(split(lines[...]), (bank_parts[0], bank_parts[1]))
         send_fwd[step // 2, 0] = parts[:ROWS, 128:]
         send_fwd[step // 2, 1] = parts[ROWS:, :128]
         send_fwd[step // 2, 2] = parts[:ROWS, :128]
-        return parts[ROWS:, 128:], exchange(step, [send_fwd.at[step // 2, s] for s in range(3)], back_devices)
-
-    def gather_sum(step, own, copies):
-        total = own
+        return parts, exchange(step, [send_fwd.at[step // 2, s] for s in range(3)], back_devices)
+
+    def gather_sum(step, parts, copies):
+        total = parts[ROWS:, 128:]
         for slot, copy in enumerate(copies):
             copy.wait_recv()
             total = total + recv[step, slot]
         return total
 
     def side_by_side(values):
-        return jnp.concatenate([values[k * CH : (k + 1) * CH] for k in range(COARSE)], axis=1)
-
-    coarse_lanes = lax.broadcasted_iota(jnp.int32, (CH, 128), 1) < 32
+        return jnp.concatenate([values[k : k + CH] for k in range(0, values.shape[0], CH)], axis=1)
 
     def mix(values, weights):
+        count, width = values.shape[0] // CH, values.shape[1]
         both = dot3(weights, split(side_by_side(values)))
-        chosen = [
-            jnp.where(coarse_lanes, both[:CH, k * 128 : (k + 1) * 128], both[CH:, k * 128 : (k + 1) * 128])
-            for k in range(COARSE)
-        ]
-        return jnp.concatenate(chosen, axis=0)
-
-    def send_mixed(step, values):
+        coarse = lax.rem(lax.broadcasted_iota(jnp.int32, both[:CH].shape, 1), 128) < 32
+        chosen = jnp.where(coarse, both[:CH], both[CH:])
+        return jnp.concatenate([chosen[:, k * width : (k + 1) * width] for k in range(count)], axis=0)
+
+    def send_next(step, values):
         send_mix[step // 2] = values
         return exchange(step, [send_mix.at[step // 2]] * 3, next_devices)
 
-    def synthesize_lines(step, copies):
+    def gather_wide(step, copies):
+        wide[ROWS:, 128:] = send_mix[step // 2]
         for copy in copies:
             copy.wait_recv()
         wide[:ROWS, :128] = recv[step, 2]
         wide[:ROWS, 128:] = recv[step, 0]
         wide[ROWS:, :128] = recv[step, 1]
-        wide[ROWS:, 128:] = send_mix[step // 2]
-        lines[...] = dot3(split(wide[...]), bank, NT)
-
+
+    loads[2].wait()
+    bank_parts[0], bank_parts[1] = split(bank_ref[...])
     for half in range(2):
         loads[half].wait()
         pack(raw, field, half)
 
     def first_column(index, carry):
-        rows, lanes = column(index)
+        rows, lanes = column_at(index)
         analyze_column(
             lambda x: field[pl.ds(pl.multiple_of(x * CH + rows, 8), 8), pl.ds(lanes, 128)], rows, lanes
         )
@@ -273,7 +311,7 @@
 
     lax.fori_loop(0, 8, first_column, 0)
     pl.semaphore_wait(barrier, nx + ny)
-    own, copies1 = send_partials(0)
+    parts, copies1 = send_partials(0)
 
     eye = (
         lax.broadcasted_iota(jnp.int32, (CH, CH), 0) == lax.broadcasted_iota(jnp.int32, (CH, CH), 1)
@@ -283,6 +321,8 @@
         form = (NT, ((), ()))
         return lax.dot_general(eye, weight, form, preferred_element_type=F32).astype(BF16)
 
+    for load in loads[3:6]:
+        load.wait()
     coarse_parts = split(wc_ref[...])
     detail_parts = split(wd_ref[...])
     skip_parts = split(ws_ref[...])
@@ -306,20 +346,20 @@
             block = slice(256 * g, 256 * g + 256)
             mixed_skip[block] = dot3(weights, split(source[block]))
 
-    loads[2].wait()
+    loads[6].wait()
     for half in range(2):
         pack(raw_cot, cot, half)
 
-    coeffs[...] = gather_sum(0, own, copies1)
-    copies2 = send_mixed(1, mix(coeffs[...], weights_forward))
+    copies2 = send_next(1, gather_sum(0, parts, copies1))
 
     skip_mix(field, 0)
 
-    synthesize_lines(1, copies2)
+    gather_wide(1, copies2)
+    lines[...] = dot3(split(mix(wide[...], weights_forward)), (bank_parts[0], bank_parts[1]), NT)
 
     def middle_column(index, carry):
-        rows, lanes = column(index)
-        walk = synthesis_column(rows, lanes)
+        rows, lanes = column_at(index)
+        walk = synthesis_column(lines, rows, lanes)
         cells = pl.ds(lanes, 128)
 
         def load(x):
@@ -337,8 +377,13 @@
         return carry
 
     lax.fori_loop(0, 8, middle_column, 0)
-    own, copies3 = send_partials(2)
-
+    parts, copies3 = send_partials(2)
+
+    flat = side_by_side(parts)
+    coarse = lax.rem(lax.broadcasted_iota(jnp.int32, flat.shape, 1), 128) < 32
+    masked = jnp.concatenate([jnp.where(coarse, flat, 0.0), jnp.where(coarse, 0.0, flat)], axis=0)
+    gsum[...] = jnp.zeros((CH, 128), F32)
+    gsum[:, :64] = dot3(split(side_by_side(wide[...])), split(masked), NT)
     pair = jnp.zeros((256, 256), F32)
     for g in range(6):
         block = slice(256 * g, 256 * g + 256)
@@ -347,17 +392,8 @@
     for i in range(1, 8):
         block = slice(i * CH, (i + 1) * CH)
         skip_sum = skip_sum + pair[block, block]
-    skip_mix(grad, 2)
-
-    back = gather_sum(2, own, copies3)
-    copies4 = send_mixed(3, mix(back, weights_back))
-
-    flat = side_by_side(back)
-    lane = lax.rem(lax.broadcasted_iota(jnp.int32, (CH, COARSE * 128), 1), 128)
-    masked = jnp.concatenate([jnp.where(lane < 32, flat, 0.0), jnp.where(lane < 32, 0.0, flat)], axis=0)
-    gsum[...] = jnp.zeros((CH, 128), F32)
-    gsum[:, :64] = dot3(split(side_by_side(coeffs[...])), split(masked), NT)
     gsum[:, 64:96] = skip_sum
+
     chunk = CH // ny
     for i in range(ny):
         ar_out[i, :chunk] = gsum[i * chunk : (i + 1) * chunk]
@@ -412,13 +448,17 @@
     ar_in[0, gy] = ar_out[gy]
     ar_start(0, source0, False)
 
+    copies4 = send_next(3, mix(gather_sum(2, parts, copies3), weights_back))
+
     ar_wait(0, source0, False)
     total = ar_sum(0, ny)
     ar_part[0] = total
     ar_in[1, gx] = total
     ar_start(1, source1, True)
 
-    synthesize_lines(3, copies4)
+    skip_mix(grad, 2)
+    base_store = pltpu.make_async_copy(mixed_skip, base_hbm, out_sems.at[0])
+    base_store.start()
 
     ar_wait(1, source1, True)
     total = ar_sum(1, nx)
@@ -426,48 +466,31 @@
     ar_in[2, gy] = total
     ar_start(2, source2, False)
 
-    stores = []
-    for half in range(2):
-
-        def last_column(index, carry):
-            rows = pl.multiple_of(index * 8, 8)
-            walk = synthesis_column(rows, 128 * half)
-            for x in range(CELLS):
-                here = pl.ds(pl.multiple_of(x * CH + rows, 8), 8)
-                value = walk.get(0, x) + mixed_skip[here, 128 * half : 128 * half + 128]
-                out[2 * half, x, pl.ds(rows, 8), :] = value[:, :CELLS]
-                out[2 * half + 1, x, pl.ds(rows, 8), :] = value[:, 64 : 64 + CELLS]
-            return carry
-
-        lax.fori_loop(0, 4, last_column, 0)
-        part = pl.ds(2 * half, 2)
-        store = pltpu.make_async_copy(out.at[part], out_hbm.at[part], out_sems.at[half])
-        store.start()
-        stores.append(store)
-
-    ar_wait(2, source2, False)
-    scale = F32(1.0 / (BATCH * CELLS * CELLS * nx * ny))
-    for i in range(ny):
-        rows = slice(i * chunk, (i + 1) * chunk)
-        values = ar_in[2, i, :chunk] * scale
-        gc_ref[rows, :] = values[:, :32]
-        gd_ref[rows, :] = values[:, 32:64]
-        gs_ref[rows, :] = values[:, 64:96]
+    gather_wide(3, copies4)
+    lines[...] = dot3(split(wide[...]), (bank_parts[0], bank_parts[1]), NT)
+    lines_store = pltpu.make_async_copy(lines, lines_hbm, out_sems.at[1])
+    lines_store.start()
 
     for copies in (copies1, copies2, copies3, copies4):
         for copy in copies:
             copy.wait_send()
     ar_wait_send(0, source0, False)
     ar_wait_send(1, source1, True)
+
+    ar_wait(2, source2, False)
+    scale = F32(1.0 / (BATCH * CELLS * CELLS * nx * ny))
+    for i in range(ny):
+        gsum[i * chunk : (i + 1) * chunk] = ar_in[2, i, :chunk] * scale
+    sum_store = pltpu.make_async_copy(gsum, sum_hbm, out_sems.at[2])
+    sum_store.start()
     ar_wait_send(2, source2, False)
-    for store in stores:
-        store.wait()
+    base_store.wait()
+    lines_store.wait()
+    sum_store.wait()
 
 
 def shards(nx, ny, field, w_coarse, w_detail, w_skip, cotangent):
     bank = bank_matrix()
-    bank_high = bank.astype(jnp.bfloat16)
-    bank_low = (bank - bank_high.astype(np.float32)).astype(jnp.bfloat16)
     block = (BATCH, CELLS, CH, CELLS)
     cells = CELLS * CH
     vmem = pl.BlockSpec(memory_space=pltpu.VMEM)
@@ -476,11 +499,16 @@
     peers = max(nx, ny)
 
 
-    result = pl.pallas_call(
+    weight = pltpu.VMEM((CH, CH), F32)
+    lines, base, summed = pl.pallas_call(
         functools.partial(kernel, nx, ny),
-        out_shape=(jax.ShapeDtypeStruct(block, F32), small, small, small),
-        in_specs=[hbm, hbm, vmem, vmem, vmem, vmem, vmem],
-        out_specs=(hbm, vmem, vmem, vmem),
+        out_shape=(
+            jax.ShapeDtypeStruct((2 * ROWS, 512), F32),
+            jax.ShapeDtypeStruct((cells, 256), F32),
+            jax.ShapeDtypeStruct((CH, 128), F32),
+        ),
+        in_specs=[hbm] * 6,
+        out_specs=(hbm, hbm, hbm),
         scratch_shapes=[
             pltpu.VMEM(block, F32),
             pltpu.VMEM(block, F32),
@@ -490,25 +518,28 @@
             pltpu.VMEM((cells, 256), F32),
             pltpu.VMEM((2 * ROWS, 512), F32),
             pltpu.VMEM((4, 256, 256), F32),
-            pltpu.VMEM(block, F32),
+            weight,
+            weight,
+            weight,
+            pltpu.VMEM((512, 256), F32),
+            pltpu.VMEM((2, 512, 256), BF16),
             pltpu.VMEM((2, 3, ROWS, 128), F32),
             pltpu.VMEM((2, ROWS, 128), F32),
             pltpu.VMEM((4, 3, ROWS, 128), F32),
-            pltpu.VMEM((ROWS, 128), F32),
             pltpu.VMEM((2 * ROWS, 256), F32),
             pltpu.VMEM((ny, 8, 128), F32),
             pltpu.VMEM((3, peers, 8, 128), F32),
             pltpu.VMEM((2, 8, 128), F32),
             pltpu.VMEM((CH, 128), F32),
+            pltpu.SemaphoreType.DMA((7,)),
             pltpu.SemaphoreType.DMA((3,)),
-            pltpu.SemaphoreType.DMA((2,)),
             pltpu.SemaphoreType.DMA((4, 3)),
             pltpu.SemaphoreType.DMA((4, 3)),
             pltpu.SemaphoreType.DMA((3, peers)),
             pltpu.SemaphoreType.DMA((3, peers)),
         ],
         compiler_params=pltpu.CompilerParams(
-            collective_id=0, has_side_effects=True, vmem_limit_bytes=48 * 1024 * 1024
+            collective_id=0, has_side_effects=True, vmem_limit_bytes=60 * 1024 * 1024
         ),
     )(
         jnp.transpose(field, (0, 1, 3, 2)),
@@ -516,9 +547,23 @@
         w_coarse,
         w_detail,
         w_skip,
-        jnp.asarray(bank_high),
-        jnp.asarray(bank_low),
+        jnp.asarray(bank),
     )
+    result = pl.pallas_call(
+        last_kernel,
+        out_shape=(jax.ShapeDtypeStruct(block, F32), small, small, small),
+        in_specs=[hbm] * 3,
+        out_specs=(hbm, vmem, vmem, vmem),
+        scratch_shapes=[
+            pltpu.VMEM((2 * ROWS, 512), F32),
+            pltpu.VMEM((cells, 256), F32),
+            pltpu.VMEM((CH, 128), F32),
+            pltpu.VMEM(block, F32),
+            pltpu.SemaphoreType.DMA((4,)),
+            pltpu.SemaphoreType.DMA((2,)),
+        ],
+        compiler_params=pltpu.CompilerParams(vmem_limit_bytes=60 * 1024 * 1024),
+    )(lines, base, summed)
     return (jnp.transpose(result[0], (0, 1, 3, 2)),) + tuple(result[1:])
 
 

time: 63.4 us -> 59.3 us (0.935)
  local copies, waits for them, and re-layouts: 7.53 us -> 0 us
  Pallas kernels: 54.8 us -> 58.5 us
    unnamed x14 -> x0, local copies, waits for them, and re-layouts: 7.53 us -> none
    pallas_call x0 -> x1, Pallas kernels: none -> 4.67 us  [shards(): pl.pallas_call(last_kernel, out_shape=(jax.ShapeDtypeStruct(block, F32),...]
    pallas_call x1, Pallas kernels: 54.8 us -> 53.8 us  [shards(): pl.pallas_call(functools.partial(kernel, nx, ny), out_shape=(jax.ShapeDty...]
where the time goes in v1:
time: 59.3 us; the launch traced here: 59.2 us
  Pallas kernels  58.5 us (99%)
  between operations  0.64 us (1%)
    pallas_call x1, Pallas kernels, shards(): pl.pallas_call(functools.partial(kernel, nx, ny), out_shape=(jax.ShapeDty...  53.8 us
    pallas_call x1, Pallas kernels, shards(): pl.pallas_call(last_kernel, out_shape=(jax.ShapeDtypeStruct(block, F32),...  4.67 us

profile of v1, /device:TPU:1, one launch (start us, length us, event | category | flops | bytes accessed | tf_op | source)
XLA Modules:
  0.0 59.2 jit_solution(2725657826028878094)
XLA Ops:
  0.6 53.8 %shard_map.93 = (f32[384,512]{1,0:T(8,128)}, f32[1536,256]{1,0:T(8,128)}, f32[32,128]{1,0:T(8,128)}) custom-call(f32[4,48,32,48]{3,2,1,0:T(8,128)} %bitcast.3, f32[4,48,32,48]{3,2,1,0:T(8,128)} %bitcast.4, f32[32,32]{1,0:T(8,128)} %wc_hbm.1, f32[32,32]{1,0:T(8,128)} %wd_hbm.1, f32[32,32]{1,0:T(8,128)} %ws_hbm.1, f32[512,256]{1,0:T(8,128)} %constant.2.clone.bank_hbm), custom_call_target="tpu_custom_call" | custom-call | tf_op jit(solution)/shard_map/pallas_call | solution.py:503
  54.5 4.7 %shard_map.94 = (f32[4,48,32,48]{3,2,1,0:T(8,128)}, f32[32,32]{1,0:T(8,128)}, f32[32,32]{1,0:T(8,128)}, f32[32,32]{1,0:T(8,128)}) custom-call(f32[384,512]{1,0:T(8,128)} %get-tuple-element.11.lines_hbm, f32[1536,256]{1,0:T(8,128)} %get-tuple-element.12.base_hbm, f32[32,128]{1,0:T(8,128)} %get-tuple-element.13.sum_hbm), custom_call_target="tpu_custom_call" | custom-call | tf_op jit(solution)/shard_map/pallas_call | solution.py:552

commit v2 on v0

v2 whole, which is shorter than its diff:
```python
import functools

import jax
import jax.numpy as jnp
import numpy as np
from jax import lax
from jax.experimental import pallas as pl
from jax.experimental.pallas import tpu as pltpu
from jax.sharding import PartitionSpec as P

LOW_TAPS = [
    0.23037781330885523,
    0.7148465705525415,
    0.6308807679295904,
    -0.02798376941698385,
    -0.18703481171888114,
    0.030841381835986965,
    0.032883011666982945,
    -0.010597401784997278,
]
HIGH_TAPS = [(-1) ** offset * LOW_TAPS[7 - offset] for offset in range(8)]

F32 = jnp.float32
BF16 = jnp.bfloat16
MESH = pl.DeviceIdType.MESH
CH = 32
BATCH = 4
CELLS = 48
COARSE = 6
ROWS = COARSE * CH // 2
GELU_A = 0.7978845608028654
GELU_B = GELU_A * 0.044715


def bounds(low, high):
    return -((7 - low) // 2), high // 2


LEVELS = [(0, CELLS - 1)]
for _ in range(3):
    LEVELS.append(bounds(*LEVELS[-1]))


def line_matrix():
    values = np.eye(CELLS)
    low, high = LEVELS[0]
    outputs = []
    for level in range(3):
        bank = [LOW_TAPS] if level < 2 else [LOW_TAPS, HIGH_TAPS]
        first, last = LEVELS[level + 1]
        outputs = []
        for taps in bank:
            result = np.zeros((last - first + 1, CELLS))
            for k in range(first, last + 1):
                for j in range(8):
                    if low <= 2 * k + j <= high:
                        result[k - first] += taps[j] * values[2 * k + j - low]
            outputs.append(result)
        values, low, high = outputs[0], first, last
    return np.stack(outputs)


def bank_matrix():
    line = line_matrix()
    result = np.zeros((2, 2, 2, 64, 2, 2, 64))
    for group in range(2):
        for xband in range(2):
            for b in range(2):
                for part in range(2):
                    for yband in range(2):
                        for k in range(COARSE):
                            lane = ((xband * 2 + yband) * COARSE + k) * 2 + b
                            result[group, xband, b, :CELLS, part, group, lane] = line[yband, part * COARSE + k]
    return result.reshape(512, 256).astype(np.float32)


def split(values):
    high = values.astype(BF16)
    return high, (values - high.astype(F32)).astype(BF16)


def dot3(left, right, dims=((1,), (0,))):
    form = (dims, ((), ()))
    total = lax.dot_general(left[0], right[0], form, preferred_element_type=F32)
    total += lax.dot_general(left[1], right[0], form, preferred_element_type=F32)
    return total + lax.dot_general(left[0], right[1], form, preferred_element_type=F32)


NT = ((1,), (1,))


class Analysis:
    def __init__(self, load):
        self.load = load
        self.memo = {}

    def get(self, level, k, taps=LOW_TAPS, band=0):
        if level == 0:
            if (0, k) not in self.memo:
                self.memo[0, k] = self.load(k)
            return self.memo[0, k]
        key = (level, k, band)
        if key not in self.memo:
            low, high = LEVELS[level - 1]
            total = None
            for j in range(8):
                if low <= 2 * k + j <= high:
                    term = self.get(level - 1, 2 * k + j) * F32(taps[j])
                    total = term if total is None else total + term
            self.memo[key] = total
        return self.memo[key]


class Synthesis:
    def __init__(self, load):
        self.load = load
        self.memo = {}

    def top(self, band, k):
        if (band, k) not in self.memo:
            self.memo[band, k] = self.load(band, k)
        return self.memo[band, k]

    def get(self, level, i):
        key = (level, i, "s")
        if key not in self.memo:
            low, high = LEVELS[level + 1]
            total = None
            for k in range(low, high + 1):
                j = i - 2 * k
                if 0 <= j < 8:
                    if level == 2:
                        term = self.top(0, k) * F32(LOW_TAPS[j]) + self.top(1, k) * F32(HIGH_TAPS[j])
                    else:
                        term = self.get(level + 1, k) * F32(LOW_TAPS[j])
                    total = term if total is None else total + term
            self.memo[key] = total
        return self.memo[key]


def synthesis_column(lines, rows):
    def load(band, k):
        part, group, row = (k + COARSE) // 6, (k + COARSE) % 6 // 3, (k + COARSE) % 3
        start = (part * 3 + row) * CH
        lanes = group * 256 + band * 128
        return lines[pl.ds(pl.multiple_of(start + rows, 8), 8), lanes : lanes + 128]

    return Synthesis(load)


def analyze_column(lines, rows, load):
    walk = Analysis(load)
    for k in range(-COARSE, COARSE):
        part, group, row = (k + COARSE) // 6, (k + COARSE) % 6 // 3, (k + COARSE) % 3
        start = (part * 3 + row) * CH
        for band, taps in enumerate((LOW_TAPS, HIGH_TAPS)):
            lanes = group * 256 + band * 128
            lines[pl.ds(pl.multiple_of(start + rows, 8), 8), lanes : lanes + 128] = walk.get(3, k, taps, band)


def side_by_side(values):
    return jnp.concatenate([values[k : k + CH] for k in range(0, values.shape[0], CH)], axis=1)


def in_coarse(values):
    return lax.rem(lax.broadcasted_iota(jnp.int32, values.shape, 1), 64) < 12


def mix(values, weights):
    count, width = values.shape[0] // CH, values.shape[1]
    both = dot3(weights, split(side_by_side(values)))
    chosen = jnp.where(in_coarse(both[:CH]), both[:CH], both[CH:])
    return jnp.concatenate([chosen[:, k * width : (k + 1) * width] for k in range(count)], axis=0)


def pack(source, target, half):
    for pair in range(2):
        values = source[2 * half + pair].reshape(CELLS * CH, CELLS)
        target[half, :, 64 * pair : 64 * pair + CELLS] = values


def kernel(
    nx, ny, field_hbm, cot_hbm, wc_hbm, wd_hbm, ws_hbm, bank_hbm, out_hbm, sum_ref,
    raw, raw_cot, field, cot, grad, skip, base, lines, kron, wc_ref, wd_ref, ws_ref, bank_ref, bank_parts,
    send_fwd, send_mix, recv, wide, out, ar_out, ar_in, ar_part, gsum,
    in_sems, out_sems, ex_send, ex_recv, ar_send, ar_recv,
):
    gx = lax.axis_index("gx")
    gy = lax.axis_index("gy")
    right, left = lax.rem(gx + 1, nx), lax.rem(gx + nx - 1, nx)
    up, down = lax.rem(gy + 1, ny), lax.rem(gy + ny - 1, ny)

    halves = [pl.ds(0, 2), pl.ds(2, 2)]
    moves = [
        (field_hbm.at[halves[0]], raw.at[halves[0]]),
        (bank_hbm, bank_ref),
        (field_hbm.at[halves[1]], raw.at[halves[1]]),
        (wc_hbm, wc_ref),
        (wd_hbm, wd_ref),
        (ws_hbm, ws_ref),
        (cot_hbm.at[halves[0]], raw_cot.at[halves[0]]),
        (cot_hbm.at[halves[1]], raw_cot.at[halves[1]]),
    ]
    loads = [pltpu.make_async_copy(source, target, in_sems.at[i]) for i, (source, target) in enumerate(moves)]
    for load in loads:
        load.start()

    barrier = pltpu.get_barrier_semaphore()

    def greet_y(r, carry):
        pl.semaphore_signal(barrier, inc=1, device_id=(gx, lax.rem(gy + r, ny)), device_id_type=MESH)
        return carry

    def greet_x(r, carry):
        pl.semaphore_signal(barrier, inc=1, device_id=(lax.rem(gx + r, nx), gy), device_id_type=MESH)
        return carry

    lax.fori_loop(1, nx, greet_x, 0)
    lax.fori_loop(1, ny, greet_y, 0)
    pl.semaphore_signal(barrier, inc=1, device_id=(right, up), device_id_type=MESH)
    pl.semaphore_signal(barrier, inc=1, device_id=(left, down), device_id_type=MESH)

    field[...] = jnp.zeros(field.shape, F32)
    cot[...] = jnp.zeros(cot.shape, F32)
    kron[...] = jnp.zeros(kron.shape, F32)

    def bank():
        return bank_parts[0], bank_parts[1]

    def exchange(step, half, sources, devices):
        copies = []
        for slot, (source, device) in enumerate(zip(sources, devices)):
            copy = pltpu.make_async_remote_copy(
                src_ref=source,
                dst_ref=recv.at[step, half, slot],
                send_sem=ex_send.at[step, half, slot],
                recv_sem=ex_recv.at[step, half, slot],
                device_id=device,
                device_id_type=MESH,
            )
            copy.start()
            copies.append(copy)
        return copies

    back_devices = [(left, gy), (gx, down), (left, down)]
    next_devices = [(right, gy), (gx, up), (right, up)]

    def send_partials(step, half):
        parts = dot3(split(lines[half]), bank())
        out_refs = send_fwd.at[step // 2, half]
        out_refs[0] = parts[:ROWS, 128:]
        out_refs[1] = parts[ROWS:, :128]
        out_refs[2] = parts[:ROWS, :128]
        return parts, exchange(step, half, [out_refs.at[s] for s in range(3)], back_devices)

    def gather_sum(step, half, parts, copies):
        total = parts[ROWS:, 128:]
        for slot, copy in enumerate(copies):
            copy.wait_recv()
            total = total + recv[step, half, slot]
        return total

    def send_next(step, half, values):
        send_mix[step // 2, half] = values
        return exchange(step, half, [send_mix.at[step // 2, half]] * 3, next_devices)

    def gather_wide(step, half, copies):
        for copy in copies:
            copy.wait_recv()
        before = jnp.concatenate([recv[step, half, 2], recv[step, half, 0]], axis=1)
        own = jnp.concatenate([recv[step, half, 1], send_mix[step // 2, half]], axis=1)
        return jnp.concatenate([before, own], axis=0)

    def cells(x, rows):
        return pl.ds(pl.multiple_of(x * CH + rows, 8), 8)

    def first(half):
        pack(raw, field, half)

        def column(index, carry):
            rows = pl.multiple_of(index * 8, 8)
            analyze_column(lines.at[half], rows, lambda x: field[half, cells(x, rows), :])
            return carry

        lax.fori_loop(0, 4, column, 0)

    loads[1].wait()
    bank_parts[0], bank_parts[1] = split(bank_ref[...])
    loads[0].wait()
    first(0)
    pl.semaphore_wait(barrier, nx + ny)
    parts0, copies1a = send_partials(0, 0)
    loads[2].wait()
    first(1)
    parts1, copies1b = send_partials(0, 1)

    eye = (
        lax.broadcasted_iota(jnp.int32, (CH, CH), 0) == lax.broadcasted_iota(jnp.int32, (CH, CH), 1)
    ).astype(BF16)

    def transposed(weight):
        form = (NT, ((), ()))
        return lax.dot_general(eye, weight, form, preferred_element_type=F32).astype(BF16)

    for load in loads[3:6]:
        load.wait()
    coarse_parts = split(wc_ref[...])
    detail_parts = split(wd_ref[...])
    skip_parts = split(ws_ref[...])
    weights_forward = tuple(
        jnp.concatenate([transposed(c), transposed(d)], axis=0) for c, d in zip(coarse_parts, detail_parts)
    )
    weights_back = tuple(jnp.concatenate([c, d], axis=0) for c, d in zip(coarse_parts, detail_parts))

    for which in range(2):
        forward = transposed(skip_parts[which]).astype(F32)
        backward = skip_parts[which].astype(F32)
        for i in range(8):
            block = slice(i * CH, (i + 1) * CH)
            kron[which, block, block] = forward
            kron[2 + which, block, block] = backward

    def skip_mix(source, target, kind, half):
        weights = (kron[kind].astype(BF16), kron[kind + 1].astype(BF16))
        for g in range(6):
            block = slice(256 * g, 256 * g + 256)
            target[half, block] = dot3(weights, split(source[half, block]))

    skip_mix(field, skip, 0, 0)
    loads[6].wait()
    pack(raw_cot, cot, 0)

    copies2a = send_next(1, 0, gather_sum(0, 0, parts0, copies1a))

    loads[7].wait()
    pack(raw_cot, cot, 1)

    copies2b = send_next(1, 1, gather_sum(0, 1, parts1, copies1b))

    skip_mix(field, skip, 0, 1)

    def middle(half, copies):
        values = gather_wide(1, half, copies)
        wide[half] = values
        lines[half] = dot3(split(mix(values, weights_forward)), bank(), NT)

        def column(index, carry):
            rows = pl.multiple_of(index * 8, 8)
            walk = synthesis_column(lines.at[half], rows)

            def load(x):
                here = cells(x, rows)
                pre = walk.get(0, x) + skip[half, here, :]
                cube = F32(GELU_B) * (pre * pre)
                tanh = jnp.tanh(pre * (F32(GELU_A) + cube))
                slope = pre * (F32(GELU_A) + F32(3.0) * cube)
                rise = (F32(0.5) + F32(0.5) * tanh) * (F32(1.0) + (slope - slope * tanh))
                value = cot[half, here, :] * rise
                grad[half, here, :] = value
                return value

            analyze_column(lines.at[half], rows, load)
            return carry

        lax.fori_loop(0, 4, column, 0)
        return send_partials(2, half)

    parts0, copies3a = middle(0, copies2a)
    parts1, copies3b = middle(1, copies2b)

    def share(half, parts):
        flat = side_by_side(parts)
        coarse = in_coarse(flat)
        masked = jnp.concatenate([jnp.where(coarse, flat, 0.0), jnp.where(coarse, 0.0, flat)], axis=0)
        both = dot3(split(side_by_side(wide[half])), split(masked), NT)
        pair = jnp.zeros((256, 256), F32)
        for g in range(6):
            block = slice(256 * g, 256 * g + 256)
            pair = pair + dot3(split(field[half, block]), split(grad[half, block]), NT)
        return both, pair

    both0, pair0 = share(0, parts0)
    copies4a = send_next(3, 0, mix(gather_sum(2, 0, parts0, copies3a), weights_back))
    both1, pair1 = share(1, parts1)

    pair = pair0 + pair1
    skip_sum = pair[:CH, :CH]
    for i in range(1, 8):
        block = slice(i * CH, (i + 1) * CH)
        skip_sum = skip_sum + pair[block, block]
    gsum[...] = jnp.zeros((CH, 128), F32)
    gsum[:, :64] = both0 + both1
    gsum[:, 64:96] = skip_sum

    chunk = CH // ny
    for i in range(ny):
        ar_out[i] = gsum[i * chunk : (i + 1) * chunk]

    def ar_copy(phase, r, source, along_x):
        size, me = (nx, gx) if along_x else (ny, gy)
        other = lax.rem(me + r, size)
        device = (other, gy) if along_x else (gx, other)
        return pltpu.make_async_remote_copy(
            src_ref=source(other),
            dst_ref=ar_in.at[phase, me],
            send_sem=ar_send.at[phase, r],
            recv_sem=ar_recv.at[phase, me],
            device_id=device,
            device_id_type=MESH,
        )

    def ar_start(phase, source, along_x):
        def step(r, carry):
            ar_copy(phase, r, source, along_x).start()
            return carry

        lax.fori_loop(1, nx if along_x else ny, step, 0)

    def ar_wait(phase, source, along_x):
        size, me = (nx, gx) if along_x else (ny, gy)

        def step(r, carry):
            other = lax.rem(me + r, size)
            arrived = ar_in.at[phase, other]
            pltpu.make_async_copy(arrived, arrived, ar_recv.at[phase, other]).wait()
            return carry

        lax.fori_loop(1, size, step, 0)

    def ar_wait_send(phase, source, along_x):
        def step(r, carry):
            ar_copy(phase, r, source, along_x).wait_send()
            return carry

        lax.fori_loop(1, nx if along_x else ny, step, 0)

    def ar_sum(phase, count):
        total = ar_in[phase, 0]
        for i in range(1, count):
            total = total + ar_in[phase, i]
        return total

    source0 = lambda other: ar_out.at[other]
    source1 = lambda other: ar_part.at[0]
    source2 = lambda other: ar_part.at[1]
    ar_in[0, gy] = ar_out[gy]
    ar_start(0, source0, False)

    skip_mix(grad, base, 2, 0)
    copies4b = send_next(3, 1, mix(gather_sum(2, 1, parts1, copies3b), weights_back))

    skip_mix(grad, base, 2, 1)

    ar_wait(0, source0, False)
    total = ar_sum(0, ny)
    ar_part[0] = total
    ar_in[1, gx] = total
    ar_start(1, source1, True)

    def last(half, copies):
        lines[half] = dot3(split(gather_wide(3, half, copies)), bank(), NT)

        def column(index, carry):
            rows = pl.multiple_of(index * 8, 8)
            walk = synthesis_column(lines.at[half], rows)
            for x in range(CELLS):
                value = walk.get(0, x) + base[half, cells(x, rows), :]
                out[2 * half, x, pl.ds(rows, 8), :] = value[:, :CELLS]
                out[2 * half + 1, x, pl.ds(rows, 8), :] = value[:, 64 : 64 + CELLS]
            return carry

        lax.fori_loop(0, 4, column, 0)
        store = pltpu.make_async_copy(out.at[halves[half]], out_hbm.at[halves[half]], out_sems.at[half])
        store.start()
        return store

    store0 = last(0, copies4a)

    ar_wait(1, source1, True)
    total = ar_sum(1, nx)
    ar_part[1] = total
    ar_in[2, gy] = total
    ar_start(2, source2, False)

    store1 = last(1, copies4b)

    for copies in (copies1a, copies1b, copies2a, copies2b, copies3a, copies3b, copies4a, copies4b):
        for copy in copies:
            copy.wait_send()
    ar_wait_send(0, source0, False)
    ar_wait_send(1, source1, True)

    ar_wait(2, source2, False)
    scale = F32(1.0 / (BATCH * CELLS * CELLS * nx * ny))
    for i in range(ny):
        sum_ref[i * chunk : (i + 1) * chunk] = ar_in[2, i] * scale
    ar_wait_send(2, source2, False)
    store0.wait()
    store1.wait()


def shards(nx, ny, field, w_coarse, w_detail, w_skip, cotangent):
    block = (BATCH, CELLS, CH, CELLS)
    packed = pltpu.VMEM((2, CELLS * CH, 128), F32)
    hbm = pl.BlockSpec(memory_space=pl.ANY)
    weight = pltpu.VMEM((CH, CH), F32)
    peers = max(nx, ny)
    chunk = CH // ny
    grad_field, summed = pl.pallas_call(
        functools.partial(kernel, nx, ny),
        out_shape=(jax.ShapeDtypeStruct(block, F32), jax.ShapeDtypeStruct((CH, 128), F32)),
        in_specs=[hbm] * 6,
        out_specs=(hbm, pl.BlockSpec(memory_space=pltpu.VMEM)),
        scratch_shapes=[
            pltpu.VMEM(block, F32),
            pltpu.VMEM(block, F32),
            packed,
            packed,
            packed,
            packed,
            packed,
            pltpu.VMEM((2, 2 * ROWS, 512), F32),
            pltpu.VMEM((4, 256, 256), F32),
            weight,
            weight,
            weight,
            pltpu.VMEM((512, 256), F32),
            pltpu.VMEM((2, 512, 256), BF16),
            pltpu.VMEM((2, 2, 3, ROWS, 128), F32),
            pltpu.VMEM((2, 2, ROWS, 128), F32),
            pltpu.VMEM((4, 2, 3, ROWS, 128), F32),
            pltpu.VMEM((2, 2 * ROWS, 256), F32),
            pltpu.VMEM(block, F32),
            pltpu.VMEM((ny, chunk, 128), F32),
            pltpu.VMEM((3, peers, chunk, 128), F32),
            pltpu.VMEM((2, chunk, 128), F32),
            pltpu.VMEM((CH, 128), F32),
            pltpu.SemaphoreType.DMA((8,)),
            pltpu.SemaphoreType.DMA((2,)),
            pltpu.SemaphoreType.DMA((4, 2, 3)),
            pltpu.SemaphoreType.DMA((4, 2, 3)),
            pltpu.SemaphoreType.DMA((3, peers)),
            pltpu.SemaphoreType.DMA((3, peers)),
        ],
        compiler_params=pltpu.CompilerParams(
            collective_id=0, has_side_effects=True, vmem_limit_bytes=60 * 1024 * 1024
        ),
    )(
        jnp.transpose(field, (0, 1, 3, 2)),
        jnp.transpose(cotangent, (0, 1, 3, 2)),
        w_coarse,
        w_detail,
        w_skip,
        jnp.asarray(bank_matrix()),
    )
    return (
        jnp.transpose(grad_field, (0, 1, 3, 2)),
        summed[:, :CH],
        summed[:, CH : 2 * CH],
        summed[:, 2 * CH : 3 * CH],
    )


def solution(mesh):
    nx, ny = mesh.shape["gx"], mesh.shape["gy"]
    in_specs = (P(None, "gx", "gy", None), P(), P(), P(), P(None, "gx", "gy", None))
    out_specs = (P(None, "gx", "gy", None), P(), P(), P())

    def run(*args):
        return shards(nx, ny, *args)

    return jax.shard_map(run, mesh=mesh, in_specs=in_specs, out_specs=out_specs, check_vma=False)
```

time: 63.4 us -> 55.2 us (0.87)
  Pallas kernels: 54.8 us -> 49 us
  local copies, waits for them, and re-layouts: 7.53 us -> 5.38 us
    pallas_call x1, Pallas kernels: 54.8 us -> 49 us  [shards(): pl.pallas_call(functools.partial(kernel, nx, ny), out_shape=(jax.ShapeDty...]
    unnamed x14 -> x1, local copies, waits for them, and re-layouts: 7.53 us -> 3.86 us
    slice x0 -> x1, local copies, waits for them, and re-layouts: none -> 1.52 us  [shards(): summed[:, 2 * CH:3 * CH]]
where the time goes in v2:
time: 55.2 us; the launch traced here: 55 us
  Pallas kernels  49 us (89%)
  local copies, waits for them, and re-layouts  5.38 us (10%)
  between operations  0.64 us (1%)
    pallas_call x1, Pallas kernels, shards(): pl.pallas_call(functools.partial(kernel, nx, ny), out_shape=(jax.ShapeDty...  49 us
    unnamed x1, local copies, waits for them, and re-layouts  3.86 us
    slice x1, local copies, waits for them, and re-layouts, shards(): summed[:, 2 * CH:3 * CH]  1.52 us

profile of v2, /device:TPU:1, one launch (start us, length us, event | category | flops | bytes accessed | tf_op | source)
XLA Modules:
  0.0 55.0 jit_solution(1687892027622852214)
XLA Ops:
  0.6 49.0 %shard_map.93 = (f32[4,48,32,48]{3,2,1,0:T(8,128)}, f32[32,128]{1,0:T(8,128)}) custom-call(f32[4,48,32,48]{3,2,1,0:T(8,128)} %bitcast.4, f32[4,48,32,48]{3,2,1,0:T(8,128)} %bitcast.5, f32[32,32]{1,0:T(8,128)} %wc_hbm.1, f32[32,32]{1,0:T(8,128)} %wd_hbm.1, f32[32,32]{1,0:T(8,128)} %ws_hbm.1, f32[512,256]{1,0:T(8,128)} %constant.2.clone.bank_hbm), custom_call_target="tpu_custom_call" | custom-call | tf_op jit(solution)/shard_map/pallas_call | solution.py:509
  49.6 1.5 %fusion = (f32[32,32]{1,0:T(8,128)}, f32[32,32]{1,0:T(8,128)}, f32[32,32]{1,0:T(8,128)}) fusion(f32[32,128]{1,0:T(8,128)} %get-tuple-element.7), kind=kLoop, calls=%fused_computation | loop fusion | bytes 24576 | tf_op jit(solution)/shard_map/slice | solution.py:560
  51.1 3.9 %copy.11 = f32[4,48,48,32]{2,3,1,0:T(8,128)} copy(f32[4,48,48,32]{2,3,1,0:T(8,128)} %bitcast.3) | data formatting | bytes 2359296

commit v3 on v2

--- a/solution.py
+++ b/solution.py
@@ -81,9 +81,9 @@
 
 def dot3(left, right, dims=((1,), (0,))):
     form = (dims, ((), ()))
-    total = lax.dot_general(left[0], right[0], form, preferred_element_type=F32)
-    total += lax.dot_general(left[1], right[0], form, preferred_element_type=F32)
-    return total + lax.dot_general(left[0], right[1], form, preferred_element_type=F32)
+    rows = left[0].shape[0]
+    both = lax.dot_general(jnp.concatenate(left, axis=0), right[0], form, preferred_element_type=F32)
+    return both[:rows] + both[rows:] + lax.dot_general(left[0], right[1], form, preferred_element_type=F32)
 
 
 NT = ((1,), (1,))
@@ -180,9 +180,9 @@
 
 
 def kernel(
-    nx, ny, field_hbm, cot_hbm, wc_hbm, wd_hbm, ws_hbm, bank_hbm, out_hbm, sum_ref,
-    raw, raw_cot, field, cot, grad, skip, base, lines, kron, wc_ref, wd_ref, ws_ref, bank_ref, bank_parts,
-    send_fwd, send_mix, recv, wide, out, ar_out, ar_in, ar_part, gsum,
+    nx, ny, field_hbm, cot_hbm, wc_hbm, wd_hbm, ws_hbm, bank_hbm, back_hbm, packed_hbm, sum_hbm,
+    raw, raw_cot, field, cot, grad, skip, base, lines, kron, wc_ref, wd_ref, ws_ref, bank_ref, bank_parts, back_ref, back_parts,
+    send_fwd, send_mix, recv, wide, packed, ar_out, ar_in, ar_part, gsum,
     in_sems, out_sems, ex_send, ex_recv, ar_send, ar_recv,
 ):
     gx = lax.axis_index("gx")
@@ -198,6 +198,7 @@
         (wc_hbm, wc_ref),
         (wd_hbm, wd_ref),
         (ws_hbm, ws_ref),
+        (back_hbm, back_ref),
         (cot_hbm.at[halves[0]], raw_cot.at[halves[0]]),
         (cot_hbm.at[halves[1]], raw_cot.at[halves[1]]),
     ]
@@ -207,18 +208,35 @@
 
     barrier = pltpu.get_barrier_semaphore()
 
-    def greet_y(r, carry):
-        pl.semaphore_signal(barrier, inc=1, device_id=(gx, lax.rem(gy + r, ny)), device_id_type=MESH)
+    across, cores = 4 if nx % 4 == 0 else nx, 2
+    near, far = across * cores, (nx // across) * (ny // cores)
+    my_x, my_y = lax.rem(gx, across), lax.div(gx, across)
+    my_core, my_z = lax.rem(gy, cores), lax.div(gy, cores)
+    near_me = my_x * cores + my_core
+    far_me = my_y * (ny // cores) + my_z
+
+    def near_device(other):
+        return my_y * across + lax.div(other, cores), my_z * cores + lax.rem(other, cores)
+
+    def far_device(other):
+        depth = ny // cores
+        return lax.div(other, depth) * across + my_x, lax.rem(other, depth) * cores + my_core
+
+    def greet(device):
+        pl.semaphore_signal(barrier, inc=1, device_id=device, device_id_type=MESH)
+
+    def greet_near(r, carry):
+        greet(near_device(lax.rem(near_me + r, near)))
         return carry
 
-    def greet_x(r, carry):
-        pl.semaphore_signal(barrier, inc=1, device_id=(lax.rem(gx + r, nx), gy), device_id_type=MESH)
+    def greet_far(r, carry):
+        greet(far_device(lax.rem(far_me + r, far)))
         return carry
 
-    lax.fori_loop(1, nx, greet_x, 0)
-    lax.fori_loop(1, ny, greet_y, 0)
-    pl.semaphore_signal(barrier, inc=1, device_id=(right, up), device_id_type=MESH)
-    pl.semaphore_signal(barrier, inc=1, device_id=(left, down), device_id_type=MESH)
+    for device in ((right, gy), (left, gy), (gx, up), (gx, down), (right, up), (left, down)):
+        greet(device)
+    lax.fori_loop(1, near, greet_near, 0)
+    lax.fori_loop(1, far, greet_far, 0)
 
     field[...] = jnp.zeros(field.shape, F32)
     cot[...] = jnp.zeros(cot.shape, F32)
@@ -226,6 +244,9 @@
 
     def bank():
         return bank_parts[0], bank_parts[1]
+
+    def bank_back():
+        return back_parts[0], back_parts[1]
 
     def exchange(step, half, sources, devices):
         copies = []
@@ -288,7 +309,7 @@
     bank_parts[0], bank_parts[1] = split(bank_ref[...])
     loads[0].wait()
     first(0)
-    pl.semaphore_wait(barrier, nx + ny)
+    pl.semaphore_wait(barrier, near + far + 4)
     parts0, copies1a = send_partials(0, 0)
     loads[2].wait()
     first(1)
@@ -302,8 +323,9 @@
         form = (NT, ((), ()))
         return lax.dot_general(eye, weight, form, preferred_element_type=F32).astype(BF16)
 
-    for load in loads[3:6]:
+    for load in loads[3:7]:
         load.wait()
+    back_parts[0], back_parts[1] = split(back_ref[...])
     coarse_parts = split(wc_ref[...])
     detail_parts = split(wd_ref[...])
     skip_parts = split(ws_ref[...])
@@ -327,12 +349,12 @@
             target[half, block] = dot3(weights, split(source[half, block]))
 
     skip_mix(field, skip, 0, 0)
-    loads[6].wait()
+    loads[7].wait()
     pack(raw_cot, cot, 0)
 
     copies2a = send_next(1, 0, gather_sum(0, 0, parts0, copies1a))
 
-    loads[7].wait()
+    loads[8].wait()
     pack(raw_cot, cot, 1)
 
     copies2b = send_next(1, 1, gather_sum(0, 1, parts1, copies1b))
@@ -342,7 +364,7 @@
     def middle(half, copies):
         values = gather_wide(1, half, copies)
         wide[half] = values
-        lines[half] = dot3(split(mix(values, weights_forward)), bank(), NT)
+        lines[half] = dot3(split(mix(values, weights_forward)), bank_back())
 
         def column(index, carry):
             rows = pl.multiple_of(index * 8, 8)
@@ -380,7 +402,6 @@
         return both, pair
 
     both0, pair0 = share(0, parts0)
-    copies4a = send_next(3, 0, mix(gather_sum(2, 0, parts0, copies3a), weights_back))
     both1, pair1 = share(1, parts1)
 
     pair = pair0 + pair1
@@ -392,14 +413,20 @@
     gsum[:, :64] = both0 + both1
     gsum[:, 64:96] = skip_sum
 
-    chunk = CH // ny
-    for i in range(ny):
+    chunk = CH // near
+    for i in range(near):
         ar_out[i] = gsum[i * chunk : (i + 1) * chunk]
 
-    def ar_copy(phase, r, source, along_x):
-        size, me = (nx, gx) if along_x else (ny, gy)
-        other = lax.rem(me + r, size)
-        device = (other, gy) if along_x else (gx, other)
+    def peer(far_round, r):
+        if far_round:
+            other = lax.rem(far_me + r, far)
+            return other, far_device(other)
+        other = lax.rem(near_me + r, near)
+        return other, near_device(other)
+
+    def ar_copy(phase, r, source):
+        other, device = peer(phase == 1, r)
+        me = far_me if phase == 1 else near_me
         return pltpu.make_async_remote_copy(
             src_ref=source(other),
             dst_ref=ar_in.at[phase, me],
@@ -409,30 +436,26 @@
             device_id_type=MESH,
         )
 
-    def ar_start(phase, source, along_x):
+    def ar_each(phase, action):
         def step(r, carry):
-            ar_copy(phase, r, source, along_x).start()
+            action(r)
             return carry
 
-        lax.fori_loop(1, nx if along_x else ny, step, 0)
-
-    def ar_wait(phase, source, along_x):
-        size, me = (nx, gx) if along_x else (ny, gy)
-
-        def step(r, carry):
-            other = lax.rem(me + r, size)
+        lax.fori_loop(1, far if phase == 1 else near, step, 0)
+
+    def ar_start(phase, source):
+        ar_each(phase, lambda r: ar_copy(phase, r, source).start())
+
+    def ar_wait(phase):
+        def action(r):
+            other, _ = peer(phase == 1, r)
             arrived = ar_in.at[phase, other]
             pltpu.make_async_copy(arrived, arrived, ar_recv.at[phase, other]).wait()
-            return carry
-
-        lax.fori_loop(1, size, step, 0)
-
-    def ar_wait_send(phase, source, along_x):
-        def step(r, carry):
-            ar_copy(phase, r, source, along_x).wait_send()
-            return carry
-
-        lax.fori_loop(1, nx if along_x else ny, step, 0)
+
+        ar_each(phase, action)
+
+    def ar_wait_send(phase, source):
+        ar_each(phase, lambda r: ar_copy(phase, r, source).wait_send())
 
     def ar_sum(phase, count):
         total = ar_in[phase, 0]
@@ -443,74 +466,119 @@
     source0 = lambda other: ar_out.at[other]
     source1 = lambda other: ar_part.at[0]
     source2 = lambda other: ar_part.at[1]
-    ar_in[0, gy] = ar_out[gy]
-    ar_start(0, source0, False)
-
+    ar_in[0, near_me] = ar_out[near_me]
+    ar_start(0, source0)
+
+    copies4a = send_next(3, 0, mix(gather_sum(2, 0, parts0, copies3a), weights_back))
     skip_mix(grad, base, 2, 0)
+
+    ar_wait(0)
+    total = ar_sum(0, near)
+    ar_part[0] = total
+    ar_in[1, far_me] = total
+    ar_start(1, source1)
+
     copies4b = send_next(3, 1, mix(gather_sum(2, 1, parts1, copies3b), weights_back))
 
     skip_mix(grad, base, 2, 1)
 
-    ar_wait(0, source0, False)
-    total = ar_sum(0, ny)
-    ar_part[0] = total
-    ar_in[1, gx] = total
-    ar_start(1, source1, True)
-
     def last(half, copies):
-        lines[half] = dot3(split(gather_wide(3, half, copies)), bank(), NT)
+        lines[half] = dot3(split(gather_wide(3, half, copies)), bank_back())
 
         def column(index, carry):
             rows = pl.multiple_of(index * 8, 8)
             walk = synthesis_column(lines.at[half], rows)
             for x in range(CELLS):
-                value = walk.get(0, x) + base[half, cells(x, rows), :]
-                out[2 * half, x, pl.ds(rows, 8), :] = value[:, :CELLS]
-                out[2 * half + 1, x, pl.ds(rows, 8), :] = value[:, 64 : 64 + CELLS]
+                packed[half, cells(x, rows), :] = walk.get(0, x) + base[half, cells(x, rows), :]
             return carry
 
         lax.fori_loop(0, 4, column, 0)
-        store = pltpu.make_async_copy(out.at[halves[half]], out_hbm.at[halves[half]], out_sems.at[half])
+        store = pltpu.make_async_copy(packed.at[half], packed_hbm.at[half], out_sems.at[half])
         store.start()
         return store
 
     store0 = last(0, copies4a)
-
-    ar_wait(1, source1, True)
-    total = ar_sum(1, nx)
+    store1 = last(1, copies4b)
+
+    ar_wait(1)
+    total = ar_sum(1, far)
     ar_part[1] = total
-    ar_in[2, gy] = total
-    ar_start(2, source2, False)
-
-    store1 = last(1, copies4b)
+    ar_in[2, near_me] = total
+    ar_start(2, source2)
 
     for copies in (copies1a, copies1b, copies2a, copies2b, copies3a, copies3b, copies4a, copies4b):
         for copy in copies:
             copy.wait_send()
-    ar_wait_send(0, source0, False)
-    ar_wait_send(1, source1, True)
-
-    ar_wait(2, source2, False)
-    scale = F32(1.0 / (BATCH * CELLS * CELLS * nx * ny))
-    for i in range(ny):
-        sum_ref[i * chunk : (i + 1) * chunk] = ar_in[2, i] * scale
-    ar_wait_send(2, source2, False)
+    ar_wait_send(0, source0)
+    ar_wait_send(1, source1)
     store0.wait()
     store1.wait()
+
+    ar_wait(2)
+    scale = F32(1.0 / (BATCH * CELLS * CELLS * nx * ny))
+    for i in range(near):
+        gsum[i * chunk : (i + 1) * chunk] = ar_in[2, i] * scale
+    store = pltpu.make_async_copy(gsum, sum_hbm, out_sems.at[2])
+    store.start()
+    ar_wait_send(2, source2)
+    store.wait()
+
+
+def unpack_kernel(packed_hbm, sum_hbm, out_hbm, gc_ref, gd_ref, gs_ref, packed, summed, out, in_sems, out_sems):
+    cells = CELLS // 2
+    rows = cells * CH
+    loads = []
+    for half in range(2):
+        for part in range(2):
+            here = pl.ds(part * rows, rows)
+            loads.append(
+                pltpu.make_async_copy(
+                    packed_hbm.at[half, here], packed.at[half, here], in_sems.at[2 * half + part]
+                )
+            )
+    loads.append(pltpu.make_async_copy(sum_hbm, summed, in_sems.at[4]))
+    for load in loads:
+        load.start()
+    stores = []
+    for half in range(2):
+        for part in range(2):
+            loads[2 * half + part].wait()
+            values = packed[half, part * rows : (part + 1) * rows]
+            there = slice(part * cells, (part + 1) * cells)
+            for pair in range(2):
+                lanes = slice(64 * pair, 64 * pair + CELLS)
+                out[2 * half + pair, there] = values[:, lanes].reshape(cells, CH, CELLS)
+            target = (pl.ds(2 * half, 2), pl.ds(part * cells, cells))
+            store = pltpu.make_async_copy(out.at[target], out_hbm.at[target], out_sems.at[2 * half + part])
+            store.start()
+            stores.append(store)
+    loads[4].wait()
+    gc_ref[...] = summed[:, :CH]
+    gd_ref[...] = summed[:, CH : 2 * CH]
+    gs_ref[...] = summed[:, 2 * CH : 3 * CH]
+    for store in stores:
+        store.wait()
 
 
 def shards(nx, ny, field, w_coarse, w_detail, w_skip, cotangent):
     block = (BATCH, CELLS, CH, CELLS)
     packed = pltpu.VMEM((2, CELLS * CH, 128), F32)
     hbm = pl.BlockSpec(memory_space=pl.ANY)
+    vmem = pl.BlockSpec(memory_space=pltpu.VMEM)
     weight = pltpu.VMEM((CH, CH), F32)
-    peers = max(nx, ny)
-    chunk = CH // ny
-    grad_field, summed = pl.pallas_call(
+    small = jax.ShapeDtypeStruct((CH, CH), F32)
+    near = 2 * (4 if nx % 4 == 0 else nx)
+    peers = max(near, nx * ny // near)
+    chunk = CH // near
+    bank = bank_matrix()
+    result, summed = pl.pallas_call(
         functools.partial(kernel, nx, ny),
-        out_shape=(jax.ShapeDtypeStruct(block, F32), jax.ShapeDtypeStruct((CH, 128), F32)),
-        in_specs=[hbm] * 6,
-        out_specs=(hbm, pl.BlockSpec(memory_space=pltpu.VMEM)),
+        out_shape=(
+            jax.ShapeDtypeStruct((2, CELLS * CH, 128), F32),
+            jax.ShapeDtypeStruct((CH, 128), F32),
+        ),
+        in_specs=[hbm] * 7,
+        out_specs=(hbm, hbm),
         scratch_shapes=[
             pltpu.VMEM(block, F32),
             pltpu.VMEM(block, F32),
@@ -526,17 +594,19 @@
             weight,
             pltpu.VMEM((512, 256), F32),
             pltpu.VMEM((2, 512, 256), BF16),
+            pltpu.VMEM((256, 512), F32),
+            pltpu.VMEM((2, 256, 512), BF16),
             pltpu.VMEM((2, 2, 3, ROWS, 128), F32),
             pltpu.VMEM((2, 2, ROWS, 128), F32),
             pltpu.VMEM((4, 2, 3, ROWS, 128), F32),
             pltpu.VMEM((2, 2 * ROWS, 256), F32),
-            pltpu.VMEM(block, F32),
-            pltpu.VMEM((ny, chunk, 128), F32),
+            packed,
+            pltpu.VMEM((near, chunk, 128), F32),
             pltpu.VMEM((3, peers, chunk, 128), F32),
             pltpu.VMEM((2, chunk, 128), F32),
             pltpu.VMEM((CH, 128), F32),
-            pltpu.SemaphoreType.DMA((8,)),
-            pltpu.SemaphoreType.DMA((2,)),
+            pltpu.SemaphoreType.DMA((9,)),
+            pltpu.SemaphoreType.DMA((3,)),
             pltpu.SemaphoreType.DMA((4, 2, 3)),
             pltpu.SemaphoreType.DMA((4, 2, 3)),
             pltpu.SemaphoreType.DMA((3, peers)),
@@ -551,14 +621,24 @@
         w_coarse,
         w_detail,
         w_skip,
-        jnp.asarray(bank_matrix()),
+        jnp.asarray(bank),
+        jnp.asarray(np.ascontiguousarray(bank.T)),
     )
-    return (
-        jnp.transpose(grad_field, (0, 1, 3, 2)),
-        summed[:, :CH],
-        summed[:, CH : 2 * CH],
-        summed[:, 2 * CH : 3 * CH],
-    )
+    grad_field, *grads = pl.pallas_call(
+        unpack_kernel,
+        out_shape=(jax.ShapeDtypeStruct(block, F32), small, small, small),
+        in_specs=[hbm, hbm],
+        out_specs=(hbm, vmem, vmem, vmem),
+        scratch_shapes=[
+            packed,
+            pltpu.VMEM((CH, 128), F32),
+            pltpu.VMEM(block, F32),
+            pltpu.SemaphoreType.DMA((5,)),
+            pltpu.SemaphoreType.DMA((4,)),
+        ],
+        compiler_params=pltpu.CompilerParams(vmem_limit_bytes=60 * 1024 * 1024),
+    )(result, summed)
+    return (jnp.transpose(grad_field, (0, 1, 3, 2)), *grads)
 
 
 def solution(mesh):

time: 55.2 us -> 51.1 us (0.926)
  local copies, waits for them, and re-layouts: 5.38 us -> 0 us
  Pallas kernels: 49 us -> 50.3 us
    unnamed x1 -> x0, local copies, waits for them, and re-layouts: 3.86 us -> none
    pallas_call x0 -> x1, Pallas kernels: none -> 3.51 us  [shards(): pl.pallas_call(unpack_kernel, out_shape=(jax.ShapeDtypeStruct(block, F32)...]
    pallas_call x1, Pallas kernels: 49 us -> 46.8 us  [shards(): pl.pallas_call(functools.partial(kernel, nx, ny), out_shape=(jax.ShapeDty...]
    slice x1 -> x0, local copies, waits for them, and re-layouts: 1.52 us -> none  [shards(): summed[:, 2 * CH:3 * CH]]
where the time goes in v3:
time: 51.1 us; the launch traced here: 51 us
  Pallas kernels  50.3 us (98%)
  between operations  0.64 us (1%)
    pallas_call x1, Pallas kernels, shards(): pl.pallas_call(functools.partial(kernel, nx, ny), out_shape=(jax.ShapeDty...  46.8 us
    pallas_call x1, Pallas kernels, shards(): pl.pallas_call(unpack_kernel, out_shape=(jax.ShapeDtypeStruct(block, F32)...  3.51 us

profile of v3, /device:TPU:1, one launch (start us, length us, event | category | flops | bytes accessed | tf_op | source)
XLA Modules:
  0.0 51.0 jit_solution(44167482769246856)
XLA Ops:
  0.6 46.8 %shard_map.102 = (f32[2,1536,128]{2,1,0:T(8,128)}, f32[32,128]{1,0:T(8,128)}) custom-call(f32[4,48,32,48]{3,2,1,0:T(8,128)} %bitcast.3, f32[4,48,32,48]{3,2,1,0:T(8,128)} %bitcast.4, f32[32,32]{1,0:T(8,128)} %wc_hbm.1, f32[32,32]{1,0:T(8,128)} %wd_hbm.1, f32[32,32]{1,0:T(8,128)} %ws_hbm.1, f32[512,256]{1,0:T(8,128)} %constant.4.clone.bank_hbm, ...), custom_call_target="tpu_custom_call" | custom-call | tf_op jit(solution)/shard_map/pallas_call | solution.py:574
  47.5 3.5 %shard_map.103 = (f32[4,48,32,48]{3,2,1,0:T(8,128)}, f32[32,32]{1,0:T(8,128)}, f32[32,32]{1,0:T(8,128)}, f32[32,32]{1,0:T(8,128)}) custom-call(f32[2,1536,128]{2,1,0:T(8,128)} %get-tuple-element.10.packed_hbm, f32[32,128]{1,0:T(8,128)} %get-tuple-element.11.sum_hbm), custom_call_target="tpu_custom_call" | custom-call | tf_op jit(solution)/shard_map/pallas_call | solution.py:627

commit v4 on v3

--- a/solution.py
+++ b/solution.py
@@ -182,7 +182,7 @@
 def kernel(
     nx, ny, field_hbm, cot_hbm, wc_hbm, wd_hbm, ws_hbm, bank_hbm, back_hbm, packed_hbm, sum_hbm,
     raw, raw_cot, field, cot, grad, skip, base, lines, kron, wc_ref, wd_ref, ws_ref, bank_ref, bank_parts, back_ref, back_parts,
-    send_fwd, send_mix, recv, wide, packed, ar_out, ar_in, ar_part, gsum,
+    send_fwd, send_mix, recv_sum, recv_next, wide, packed, ar_out, ar_in, ar_part, gsum,
     in_sems, out_sems, ex_send, ex_recv, ar_send, ar_recv,
 ):
     gx = lax.axis_index("gx")
@@ -233,7 +233,9 @@
         greet(far_device(lax.rem(far_me + r, far)))
         return carry
 
-    for device in ((right, gy), (left, gy), (gx, up), (gx, down), (right, up), (left, down)):
+    for device in ((right, gy), (left, gy), (gx, up), (gx, down)):
+        greet(device)
+    for device in ((right, up), (left, down), (right, down), (left, up)):
         greet(device)
     lax.fori_loop(1, near, greet_near, 0)
     lax.fori_loop(1, far, greet_far, 0)
@@ -248,12 +250,12 @@
     def bank_back():
         return back_parts[0], back_parts[1]
 
-    def exchange(step, half, sources, devices):
+    def exchange(step, half, moves):
         copies = []
-        for slot, (source, device) in enumerate(zip(sources, devices)):
+        for slot, (source, target, device) in enumerate(moves):
             copy = pltpu.make_async_remote_copy(
                 src_ref=source,
-                dst_ref=recv.at[step, half, slot],
+                dst_ref=target,
                 send_sem=ex_send.at[step, half, slot],
                 recv_sem=ex_recv.at[step, half, slot],
                 device_id=device,
@@ -263,34 +265,39 @@
             copies.append(copy)
         return copies
 
-    back_devices = [(left, gy), (gx, down), (left, down)]
-    next_devices = [(right, gy), (gx, up), (right, up)]
-
     def send_partials(step, half):
         parts = dot3(split(lines[half]), bank())
-        out_refs = send_fwd.at[step // 2, half]
-        out_refs[0] = parts[:ROWS, 128:]
-        out_refs[1] = parts[ROWS:, :128]
-        out_refs[2] = parts[:ROWS, :128]
-        return parts, exchange(step, half, [out_refs.at[s] for s in range(3)], back_devices)
+        before, own = send_fwd.at[step // 2, half, 0], send_fwd.at[step // 2, half, 1]
+        before[...] = parts[:, :128]
+        own[...] = parts[:, 128:]
+        arrived = recv_sum.at[step // 2, half]
+        first, second = pl.ds(0, ROWS), pl.ds(ROWS, ROWS)
+        moves = [
+            (before.at[first], arrived.at[pl.ds(0, ROWS)], (left, down)),
+            (before.at[second], arrived.at[pl.ds(ROWS, ROWS)], (right, down)),
+            (own.at[first], arrived.at[pl.ds(2 * ROWS, ROWS)], (left, gy)),
+            (own.at[second], arrived.at[pl.ds(3 * ROWS, ROWS)], (right, gy)),
+            (before, arrived.at[pl.ds(4 * ROWS, 2 * ROWS)], (gx, down)),
+        ]
+        return parts, exchange(step, half, moves)
 
     def gather_sum(step, half, parts, copies):
-        total = parts[ROWS:, 128:]
-        for slot, copy in enumerate(copies):
+        for copy in copies:
             copy.wait_recv()
-            total = total + recv[step, half, slot]
-        return total
+        arrived = recv_sum[step // 2, half]
+        total = parts[:, 128:] + arrived[4 * ROWS :]
+        above = arrived[ROWS : 2 * ROWS] + arrived[3 * ROWS : 4 * ROWS]
+        below = arrived[:ROWS] + arrived[2 * ROWS : 3 * ROWS]
+        return total + jnp.concatenate([above, below], axis=0)
 
     def send_next(step, half, values):
         send_mix[step // 2, half] = values
-        return exchange(step, half, [send_mix.at[step // 2, half]] * 3, next_devices)
+        return exchange(step, half, [(send_mix.at[step // 2, half], recv_next.at[step // 2, half], (gx, up))])
 
     def gather_wide(step, half, copies):
         for copy in copies:
             copy.wait_recv()
-        before = jnp.concatenate([recv[step, half, 2], recv[step, half, 0]], axis=1)
-        own = jnp.concatenate([recv[step, half, 1], send_mix[step // 2, half]], axis=1)
-        return jnp.concatenate([before, own], axis=0)
+        return jnp.concatenate([recv_next[step // 2, half], send_mix[step // 2, half]], axis=1)
 
     def cells(x, rows):
         return pl.ds(pl.multiple_of(x * CH + rows, 8), 8)
@@ -309,7 +316,7 @@
     bank_parts[0], bank_parts[1] = split(bank_ref[...])
     loads[0].wait()
     first(0)
-    pl.semaphore_wait(barrier, near + far + 4)
+    pl.semaphore_wait(barrier, near + far + 6)
     parts0, copies1a = send_partials(0, 0)
     loads[2].wait()
     first(1)
@@ -524,7 +531,9 @@
     store.wait()
 
 
-def unpack_kernel(packed_hbm, sum_hbm, out_hbm, gc_ref, gd_ref, gs_ref, packed, summed, out, in_sems, out_sems):
+def unpack_kernel(
+    packed_hbm, sum_hbm, out_hbm, gc_hbm, gd_hbm, gs_hbm, packed, summed, grads, out, in_sems, out_sems
+):
     cells = CELLS // 2
     rows = cells * CH
     loads = []
@@ -537,9 +546,15 @@
                 )
             )
     loads.append(pltpu.make_async_copy(sum_hbm, summed, in_sems.at[4]))
-    for load in loads:
+    for load in loads[4:] + loads[:4]:
         load.start()
     stores = []
+    loads[4].wait()
+    for i, target in enumerate((gc_hbm, gd_hbm, gs_hbm)):
+        grads[i] = summed[:, i * CH : (i + 1) * CH]
+        store = pltpu.make_async_copy(grads.at[i], target, out_sems.at[4 + i])
+        store.start()
+        stores.append(store)
     for half in range(2):
         for part in range(2):
             loads[2 * half + part].wait()
@@ -552,10 +567,6 @@
             store = pltpu.make_async_copy(out.at[target], out_hbm.at[target], out_sems.at[2 * half + part])
             store.start()
             stores.append(store)
-    loads[4].wait()
-    gc_ref[...] = summed[:, :CH]
-    gd_ref[...] = summed[:, CH : 2 * CH]
-    gs_ref[...] = summed[:, 2 * CH : 3 * CH]
     for store in stores:
         store.wait()
 
@@ -564,7 +575,6 @@
     block = (BATCH, CELLS, CH, CELLS)
     packed = pltpu.VMEM((2, CELLS * CH, 128), F32)
     hbm = pl.BlockSpec(memory_space=pl.ANY)
-    vmem = pl.BlockSpec(memory_space=pltpu.VMEM)
     weight = pltpu.VMEM((CH, CH), F32)
     small = jax.ShapeDtypeStruct((CH, CH), F32)
     near = 2 * (4 if nx % 4 == 0 else nx)
@@ -596,9 +606,10 @@
             pltpu.VMEM((2, 512, 256), BF16),
             pltpu.VMEM((256, 512), F32),
             pltpu.VMEM((2, 256, 512), BF16),
-            pltpu.VMEM((2, 2, 3, ROWS, 128), F32),
-            pltpu.VMEM((2, 2, ROWS, 128), F32),
-            pltpu.VMEM((4, 2, 3, ROWS, 128), F32),
+            pltpu.VMEM((2, 2, 2, 2 * ROWS, 128), F32),
+            pltpu.VMEM((2, 2, 2 * ROWS, 128), F32),
+            pltpu.VMEM((2, 2, 6 * ROWS, 128), F32),
+            pltpu.VMEM((2, 2, 2 * ROWS, 128), F32),
             pltpu.VMEM((2, 2 * ROWS, 256), F32),
             packed,
             pltpu.VMEM((near, chunk, 128), F32),
@@ -607,8 +618,8 @@
             pltpu.VMEM((CH, 128), F32),
             pltpu.SemaphoreType.DMA((9,)),
             pltpu.SemaphoreType.DMA((3,)),
-            pltpu.SemaphoreType.DMA((4, 2, 3)),
-            pltpu.SemaphoreType.DMA((4, 2, 3)),
+            pltpu.SemaphoreType.DMA((4, 2, 5)),
+            pltpu.SemaphoreType.DMA((4, 2, 5)),
             pltpu.SemaphoreType.DMA((3, peers)),
             pltpu.SemaphoreType.DMA((3, peers)),
         ],
@@ -628,13 +639,14 @@
         unpack_kernel,
         out_shape=(jax.ShapeDtypeStruct(block, F32), small, small, small),
         in_specs=[hbm, hbm],
-        out_specs=(hbm, vmem, vmem, vmem),
+        out_specs=(hbm, hbm, hbm, hbm),
         scratch_shapes=[
             packed,
             pltpu.VMEM((CH, 128), F32),
+            pltpu.VMEM((3, CH, CH), F32),
             pltpu.VMEM(block, F32),
             pltpu.SemaphoreType.DMA((5,)),
-            pltpu.SemaphoreType.DMA((4,)),
+            pltpu.SemaphoreType.DMA((7,)),
         ],
         compiler_params=pltpu.CompilerParams(vmem_limit_bytes=60 * 1024 * 1024),
     )(result, summed)

time: 51.1 us -> 48.9 us (0.957)
  Pallas kernels: 50.3 us -> 48.1 us
    pallas_call x1, Pallas kernels: 46.8 us -> 45.1 us  [shards(): pl.pallas_call(functools.partial(kernel, nx, ny), out_shape=(jax.ShapeDty...]
    pallas_call x1, Pallas kernels: 3.51 us -> 2.94 us  [shards(): pl.pallas_call(unpack_kernel, out_shape=(jax.ShapeDtypeStruct(block, F32)...]
where the time goes in v4:
time: 48.9 us; the launch traced here: 48.7 us
  Pallas kernels  48.1 us (98%)
  between operations  0.64 us (1%)
    pallas_call x1, Pallas kernels, shards(): pl.pallas_call(functools.partial(kernel, nx, ny), out_shape=(jax.ShapeDty...  45.1 us
    pallas_call x1, Pallas kernels, shards(): pl.pallas_call(unpack_kernel, out_shape=(jax.ShapeDtypeStruct(block, F32)...  2.94 us

profile of v4, /device:TPU:1, one launch (start us, length us, event | category | flops | bytes accessed | tf_op | source)
XLA Modules:
  0.0 48.7 jit_solution(8946284785308606003)
XLA Ops:
  0.6 45.1 %shard_map.102 = (f32[2,1536,128]{2,1,0:T(8,128)}, f32[32,128]{1,0:T(8,128)}) custom-call(f32[4,48,32,48]{3,2,1,0:T(8,128)} %bitcast.3, f32[4,48,32,48]{3,2,1,0:T(8,128)} %bitcast.4, f32[32,32]{1,0:T(8,128)} %wc_hbm.1, f32[32,32]{1,0:T(8,128)} %wd_hbm.1, f32[32,32]{1,0:T(8,128)} %ws_hbm.1, f32[512,256]{1,0:T(8,128)} %constant.4.clone.bank_hbm, ...), custom_call_target="tpu_custom_call" | custom-call | tf_op jit(solution)/shard_map/pallas_call | solution.py:584
  45.8 2.9 %shard_map.103 = (f32[4,48,32,48]{3,2,1,0:T(8,128)}, f32[32,32]{1,0:T(8,128)}, f32[32,32]{1,0:T(8,128)}, f32[32,32]{1,0:T(8,128)}) custom-call(f32[2,1536,128]{2,1,0:T(8,128)} %get-tuple-element.10.packed_hbm, f32[32,128]{1,0:T(8,128)} %get-tuple-element.11.sum_hbm), custom_call_target="tpu_custom_call" | custom-call | tf_op jit(solution)/shard_map/pallas_call | solution.py:638

commit v5 on v4

--- a/solution.py
+++ b/solution.py
@@ -182,8 +182,8 @@
 def kernel(
     nx, ny, field_hbm, cot_hbm, wc_hbm, wd_hbm, ws_hbm, bank_hbm, back_hbm, packed_hbm, sum_hbm,
     raw, raw_cot, field, cot, grad, skip, base, lines, kron, wc_ref, wd_ref, ws_ref, bank_ref, bank_parts, back_ref, back_parts,
-    send_fwd, send_mix, recv_sum, recv_next, wide, packed, ar_out, ar_in, ar_part, gsum,
-    in_sems, out_sems, ex_send, ex_recv, ar_send, ar_recv,
+    send_fwd, send_mix, recv_sum, recv_next, wide, packed, ar_pair, ar_in, ar_part, gsum, result,
+    in_sems, out_sems, ex_send, ex_recv, ar_send, ar_recv, pair_send, pair_recv,
 ):
     gx = lax.axis_index("gx")
     gy = lax.axis_index("gy")
@@ -208,37 +208,35 @@
 
     barrier = pltpu.get_barrier_semaphore()
 
-    across, cores = 4 if nx % 4 == 0 else nx, 2
-    near, far = across * cores, (nx // across) * (ny // cores)
-    my_x, my_y = lax.rem(gx, across), lax.div(gx, across)
-    my_core, my_z = lax.rem(gy, cores), lax.div(gy, cores)
-    near_me = my_x * cores + my_core
-    far_me = my_y * (ny // cores) + my_z
-
-    def near_device(other):
-        return my_y * across + lax.div(other, cores), my_z * cores + lax.rem(other, cores)
-
-    def far_device(other):
-        depth = ny // cores
-        return lax.div(other, depth) * across + my_x, lax.rem(other, depth) * cores + my_core
+    core, depth = lax.rem(gy, 2), ny // 2
+    my_z = lax.div(gy, 2)
+    partner = (gx, gy + 1 - 2 * core)
+
+    def line(axis):
+        if axis == 0:
+            return nx, gx, lambda other: (other, gy)
+        return depth, my_z, lambda other: (gx, other * 2 + core)
 
     def greet(device):
         pl.semaphore_signal(barrier, inc=1, device_id=device, device_id_type=MESH)
 
-    def greet_near(r, carry):
-        greet(near_device(lax.rem(near_me + r, near)))
-        return carry
-
-    def greet_far(r, carry):
-        greet(far_device(lax.rem(far_me + r, far)))
-        return carry
+    def each(axis, action):
+        size, me, device = line(axis)
+
+        def step(r, carry):
+            other = lax.rem(me + r, size)
+            action(r, other, device(other))
+            return carry
+
+        lax.fori_loop(1, size, step, 0)
 
     for device in ((right, gy), (left, gy), (gx, up), (gx, down)):
         greet(device)
     for device in ((right, up), (left, down), (right, down), (left, up)):
         greet(device)
-    lax.fori_loop(1, near, greet_near, 0)
-    lax.fori_loop(1, far, greet_far, 0)
+    greet(partner)
+    for axis in range(2):
+        each(axis, lambda r, other, device: greet(device))
 
     field[...] = jnp.zeros(field.shape, F32)
     cot[...] = jnp.zeros(cot.shape, F32)
@@ -316,7 +314,7 @@
     bank_parts[0], bank_parts[1] = split(bank_ref[...])
     loads[0].wait()
     first(0)
-    pl.semaphore_wait(barrier, near + far + 6)
+    pl.semaphore_wait(barrier, 8 + 1 + nx - 1 + depth - 1)
     parts0, copies1a = send_partials(0, 0)
     loads[2].wait()
     first(1)
@@ -416,75 +414,56 @@
     for i in range(1, 8):
         block = slice(i * CH, (i + 1) * CH)
         skip_sum = skip_sum + pair[block, block]
-    gsum[...] = jnp.zeros((CH, 128), F32)
-    gsum[:, :64] = both0 + both1
-    gsum[:, 64:96] = skip_sum
-
-    chunk = CH // near
-    for i in range(near):
-        ar_out[i] = gsum[i * chunk : (i + 1) * chunk]
-
-    def peer(far_round, r):
-        if far_round:
-            other = lax.rem(far_me + r, far)
-            return other, far_device(other)
-        other = lax.rem(near_me + r, near)
-        return other, near_device(other)
-
-    def ar_copy(phase, r, source):
-        other, device = peer(phase == 1, r)
-        me = far_me if phase == 1 else near_me
+    share_sum = jnp.concatenate([both0 + both1, skip_sum, jnp.zeros((CH, CH), F32)], axis=1)
+    gsum[0] = share_sum[: CH // 2]
+    gsum[1] = share_sum[CH // 2 :]
+
+    def to_partner(phase, source, target):
         return pltpu.make_async_remote_copy(
-            src_ref=source(other),
-            dst_ref=ar_in.at[phase, me],
-            send_sem=ar_send.at[phase, r],
-            recv_sem=ar_recv.at[phase, me],
+            src_ref=source,
+            dst_ref=target,
+            send_sem=pair_send.at[phase],
+            recv_sem=pair_recv.at[phase],
+            device_id=partner,
+            device_id_type=MESH,
+        )
+
+    def line_copy(axis, r, device):
+        me = line(axis)[1]
+        return pltpu.make_async_remote_copy(
+            src_ref=ar_part.at[axis],
+            dst_ref=ar_in.at[axis, me],
+            send_sem=ar_send.at[axis, r],
+            recv_sem=ar_recv.at[axis, me],
             device_id=device,
             device_id_type=MESH,
         )
 
-    def ar_each(phase, action):
-        def step(r, carry):
-            action(r)
-            return carry
-
-        lax.fori_loop(1, far if phase == 1 else near, step, 0)
-
-    def ar_start(phase, source):
-        ar_each(phase, lambda r: ar_copy(phase, r, source).start())
-
-    def ar_wait(phase):
-        def action(r):
-            other, _ = peer(phase == 1, r)
-            arrived = ar_in.at[phase, other]
-            pltpu.make_async_copy(arrived, arrived, ar_recv.at[phase, other]).wait()
-
-        ar_each(phase, action)
-
-    def ar_wait_send(phase, source):
-        ar_each(phase, lambda r: ar_copy(phase, r, source).wait_send())
-
-    def ar_sum(phase, count):
-        total = ar_in[phase, 0]
-        for i in range(1, count):
-            total = total + ar_in[phase, i]
+    def line_start(axis, total):
+        ar_part[axis] = total
+        ar_in[axis, line(axis)[1]] = total
+        each(axis, lambda r, other, device: line_copy(axis, r, device).start())
+
+    def line_sum(axis):
+        def arrive(r, other, device):
+            arrived = ar_in.at[axis, other]
+            pltpu.make_async_copy(arrived, arrived, ar_recv.at[axis, other]).wait()
+
+        each(axis, arrive)
+        total = ar_in[axis, 0]
+        for i in range(1, line(axis)[0]):
+            total = total + ar_in[axis, i]
         return total
 
-    source0 = lambda other: ar_out.at[other]
-    source1 = lambda other: ar_part.at[0]
-    source2 = lambda other: ar_part.at[1]
-    ar_in[0, near_me] = ar_out[near_me]
-    ar_start(0, source0)
+    swap = to_partner(0, gsum.at[1 - core], ar_pair)
+    swap.start()
 
     copies4a = send_next(3, 0, mix(gather_sum(2, 0, parts0, copies3a), weights_back))
+
+    swap.wait_recv()
+    line_start(0, gsum[core] + ar_pair[...])
+
     skip_mix(grad, base, 2, 0)
-
-    ar_wait(0)
-    total = ar_sum(0, near)
-    ar_part[0] = total
-    ar_in[1, far_me] = total
-    ar_start(1, source1)
-
     copies4b = send_next(3, 1, mix(gather_sum(2, 1, parts1, copies3b), weights_back))
 
     skip_mix(grad, base, 2, 1)
@@ -505,29 +484,27 @@
         return store
 
     store0 = last(0, copies4a)
+    line_start(1, line_sum(0))
+
     store1 = last(1, copies4b)
 
-    ar_wait(1)
-    total = ar_sum(1, far)
-    ar_part[1] = total
-    ar_in[2, near_me] = total
-    ar_start(2, source2)
+    scale = F32(1.0 / (BATCH * CELLS * CELLS * nx * ny))
+    result[core] = line_sum(1) * scale
+    swap_back = to_partner(1, result.at[core], result.at[core])
+    swap_back.start()
 
     for copies in (copies1a, copies1b, copies2a, copies2b, copies3a, copies3b, copies4a, copies4b):
         for copy in copies:
             copy.wait_send()
-    ar_wait_send(0, source0)
-    ar_wait_send(1, source1)
+    for axis in range(2):
+        each(axis, lambda r, other, device: line_copy(axis, r, device).wait_send())
+    swap.wait_send()
     store0.wait()
     store1.wait()
 
-    ar_wait(2)
-    scale = F32(1.0 / (BATCH * CELLS * CELLS * nx * ny))
-    for i in range(near):
-        gsum[i * chunk : (i + 1) * chunk] = ar_in[2, i] * scale
-    store = pltpu.make_async_copy(gsum, sum_hbm, out_sems.at[2])
+    swap_back.wait()
+    store = pltpu.make_async_copy(result, sum_hbm, out_sems.at[2])
     store.start()
-    ar_wait_send(2, source2)
     store.wait()
 
 
@@ -551,7 +528,9 @@
     stores = []
     loads[4].wait()
     for i, target in enumerate((gc_hbm, gd_hbm, gs_hbm)):
-        grads[i] = summed[:, i * CH : (i + 1) * CH]
+        for part in range(2):
+            rows_here = slice(part * CH // 2, (part + 1) * CH // 2)
+            grads[i, rows_here] = summed[part, :, i * CH : (i + 1) * CH]
         store = pltpu.make_async_copy(grads.at[i], target, out_sems.at[4 + i])
         store.start()
         stores.append(store)
@@ -577,15 +556,14 @@
     hbm = pl.BlockSpec(memory_space=pl.ANY)
     weight = pltpu.VMEM((CH, CH), F32)
     small = jax.ShapeDtypeStruct((CH, CH), F32)
-    near = 2 * (4 if nx % 4 == 0 else nx)
-    peers = max(near, nx * ny // near)
-    chunk = CH // near
+    peers = max(nx, ny // 2)
+    half_sum = (CH // 2, 128)
     bank = bank_matrix()
-    result, summed = pl.pallas_call(
+    packed_field, summed = pl.pallas_call(
         functools.partial(kernel, nx, ny),
         out_shape=(
             jax.ShapeDtypeStruct((2, CELLS * CH, 128), F32),
-            jax.ShapeDtypeStruct((CH, 128), F32),
+            jax.ShapeDtypeStruct((2, *half_sum), F32),
         ),
         in_specs=[hbm] * 7,
         out_specs=(hbm, hbm),
@@ -612,16 +590,19 @@
             pltpu.VMEM((2, 2, 2 * ROWS, 128), F32),
             pltpu.VMEM((2, 2 * ROWS, 256), F32),
             packed,
-            pltpu.VMEM((near, chunk, 128), F32),
-            pltpu.VMEM((3, peers, chunk, 128), F32),
-            pltpu.VMEM((2, chunk, 128), F32),
-            pltpu.VMEM((CH, 128), F32),
+            pltpu.VMEM(half_sum, F32),
+            pltpu.VMEM((2, peers, *half_sum), F32),
+            pltpu.VMEM((2, *half_sum), F32),
+            pltpu.VMEM((2, *half_sum), F32),
+            pltpu.VMEM((2, *half_sum), F32),
             pltpu.SemaphoreType.DMA((9,)),
             pltpu.SemaphoreType.DMA((3,)),
             pltpu.SemaphoreType.DMA((4, 2, 5)),
             pltpu.SemaphoreType.DMA((4, 2, 5)),
-            pltpu.SemaphoreType.DMA((3, peers)),
-            pltpu.SemaphoreType.DMA((3, peers)),
+            pltpu.SemaphoreType.DMA((2, peers)),
+            pltpu.SemaphoreType.DMA((2, peers)),
+            pltpu.SemaphoreType.DMA((2,)),
+            pltpu.SemaphoreType.DMA((2,)),
         ],
         compiler_params=pltpu.CompilerParams(
             collective_id=0, has_side_effects=True, vmem_limit_bytes=60 * 1024 * 1024
@@ -642,14 +623,14 @@
         out_specs=(hbm, hbm, hbm, hbm),
         scratch_shapes=[
             packed,
-            pltpu.VMEM((CH, 128), F32),
+            pltpu.VMEM((2, *half_sum), F32),
             pltpu.VMEM((3, CH, CH), F32),
             pltpu.VMEM(block, F32),
             pltpu.SemaphoreType.DMA((5,)),
             pltpu.SemaphoreType.DMA((7,)),
         ],
         compiler_params=pltpu.CompilerParams(vmem_limit_bytes=60 * 1024 * 1024),
-    )(result, summed)
+    )(packed_field, summed)
     return (jnp.transpose(grad_field, (0, 1, 3, 2)), *grads)
 
 

time: 48.9 us -> 46.5 us (0.951)
  Pallas kernels: 48.1 us -> 45.6 us
    pallas_call x1, Pallas kernels: 45.1 us -> 42.7 us  [shards(): pl.pallas_call(functools.partial(kernel, nx, ny), out_shape=(jax.ShapeDty...]
where the time goes in v5:
time: 46.5 us; the launch traced here: 46.3 us
  Pallas kernels  45.6 us (98%)
  between operations  0.64 us (1%)
    pallas_call x1, Pallas kernels, shards(): pl.pallas_call(functools.partial(kernel, nx, ny), out_shape=(jax.ShapeDty...  42.7 us
    pallas_call x1, Pallas kernels, shards(): pl.pallas_call(unpack_kernel, out_shape=(jax.ShapeDtypeStruct(block, F32)...  2.94 us

profile of v5, /device:TPU:1, one launch (start us, length us, event | category | flops | bytes accessed | tf_op | source)
XLA Modules:
  0.0 46.3 jit_solution(15876389698298506146)
XLA Ops:
  0.6 42.7 %shard_map.102 = (f32[2,1536,128]{2,1,0:T(8,128)}, f32[2,16,128]{2,1,0:T(8,128)}) custom-call(f32[4,48,32,48]{3,2,1,0:T(8,128)} %bitcast.3, f32[4,48,32,48]{3,2,1,0:T(8,128)} %bitcast.4, f32[32,32]{1,0:T(8,128)} %wc_hbm.1, f32[32,32]{1,0:T(8,128)} %wd_hbm.1, f32[32,32]{1,0:T(8,128)} %ws_hbm.1, f32[512,256]{1,0:T(8,128)} %constant.4.clone.bank_hbm, ...), custom_call_target="tpu_custom_call" | custom-call | tf_op jit(solution)/shard_map/pallas_call | solution.py:562
  43.3 2.9 %shard_map.103 = (f32[4,48,32,48]{3,2,1,0:T(8,128)}, f32[32,32]{1,0:T(8,128)}, f32[32,32]{1,0:T(8,128)}, f32[32,32]{1,0:T(8,128)}) custom-call(f32[2,1536,128]{2,1,0:T(8,128)} %get-tuple-element.10.packed_hbm, f32[2,16,128]{2,1,0:T(8,128)} %get-tuple-element.11.sum_hbm), custom_call_target="tpu_custom_call" | custom-call | tf_op jit(solution)/shard_map/pallas_call | solution.py:619

commit v6 on v5

--- a/solution.py
+++ b/solution.py
@@ -190,18 +190,15 @@
     right, left = lax.rem(gx + 1, nx), lax.rem(gx + nx - 1, nx)
     up, down = lax.rem(gy + 1, ny), lax.rem(gy + ny - 1, ny)
 
-    halves = [pl.ds(0, 2), pl.ds(2, 2)]
-    moves = [
-        (field_hbm.at[halves[0]], raw.at[halves[0]]),
-        (bank_hbm, bank_ref),
-        (field_hbm.at[halves[1]], raw.at[halves[1]]),
-        (wc_hbm, wc_ref),
-        (wd_hbm, wd_ref),
-        (ws_hbm, ws_ref),
-        (back_hbm, back_ref),
-        (cot_hbm.at[halves[0]], raw_cot.at[halves[0]]),
-        (cot_hbm.at[halves[1]], raw_cot.at[halves[1]]),
-    ]
+    def piece(source, target, b, part):
+        here = (b, pl.ds(part * (CELLS // 2), CELLS // 2))
+        return source.at[here], target.at[here]
+
+    moves = [piece(field_hbm, raw, b, part) for b in range(2) for part in range(2)]
+    moves += [(bank_hbm, bank_ref)]
+    moves += [piece(field_hbm, raw, b, part) for b in range(2, 4) for part in range(2)]
+    moves += [(wc_hbm, wc_ref), (wd_hbm, wd_ref), (ws_hbm, ws_ref), (back_hbm, back_ref)]
+    moves += [(cot_hbm.at[pl.ds(2 * half, 2)], raw_cot.at[pl.ds(2 * half, 2)]) for half in range(2)]
     loads = [pltpu.make_async_copy(source, target, in_sems.at[i]) for i, (source, target) in enumerate(moves)]
     for load in loads:
         load.start()
@@ -239,8 +236,6 @@
         each(axis, lambda r, other, device: greet(device))
 
     field[...] = jnp.zeros(field.shape, F32)
-    cot[...] = jnp.zeros(cot.shape, F32)
-    kron[...] = jnp.zeros(kron.shape, F32)
 
     def bank():
         return bank_parts[0], bank_parts[1]
@@ -301,7 +296,13 @@
         return pl.ds(pl.multiple_of(x * CH + rows, 8), 8)
 
     def first(half):
-        pack(raw, field, half)
+        for pair in range(2):
+            for part in range(2):
+                loads[5 * half + 2 * pair + part].wait()
+                here = slice(part * (CELLS // 2), (part + 1) * (CELLS // 2))
+                rows = slice(part * (CELLS // 2) * CH, (part + 1) * (CELLS // 2) * CH)
+                values = raw[2 * half + pair, here].reshape(CELLS // 2 * CH, CELLS)
+                field[half, rows, 64 * pair : 64 * pair + CELLS] = values
 
         def column(index, carry):
             rows = pl.multiple_of(index * 8, 8)
@@ -310,13 +311,11 @@
 
         lax.fori_loop(0, 4, column, 0)
 
-    loads[1].wait()
+    first(0)
+    loads[4].wait()
     bank_parts[0], bank_parts[1] = split(bank_ref[...])
-    loads[0].wait()
-    first(0)
     pl.semaphore_wait(barrier, 8 + 1 + nx - 1 + depth - 1)
     parts0, copies1a = send_partials(0, 0)
-    loads[2].wait()
     first(1)
     parts1, copies1b = send_partials(0, 1)
 
@@ -328,7 +327,7 @@
         form = (NT, ((), ()))
         return lax.dot_general(eye, weight, form, preferred_element_type=F32).astype(BF16)
 
-    for load in loads[3:7]:
+    for load in loads[9:13]:
         load.wait()
     back_parts[0], back_parts[1] = split(back_ref[...])
     coarse_parts = split(wc_ref[...])
@@ -339,6 +338,8 @@
     )
     weights_back = tuple(jnp.concatenate([c, d], axis=0) for c, d in zip(coarse_parts, detail_parts))
 
+    cot[...] = jnp.zeros(cot.shape, F32)
+    kron[...] = jnp.zeros(kron.shape, F32)
     for which in range(2):
         forward = transposed(skip_parts[which]).astype(F32)
         backward = skip_parts[which].astype(F32)
@@ -354,12 +355,12 @@
             target[half, block] = dot3(weights, split(source[half, block]))
 
     skip_mix(field, skip, 0, 0)
-    loads[7].wait()
+    loads[13].wait()
     pack(raw_cot, cot, 0)
 
     copies2a = send_next(1, 0, gather_sum(0, 0, parts0, copies1a))
 
-    loads[8].wait()
+    loads[14].wait()
     pack(raw_cot, cot, 1)
 
     copies2b = send_next(1, 1, gather_sum(0, 1, parts1, copies1b))
@@ -400,21 +401,12 @@
         coarse = in_coarse(flat)
         masked = jnp.concatenate([jnp.where(coarse, flat, 0.0), jnp.where(coarse, 0.0, flat)], axis=0)
         both = dot3(split(side_by_side(wide[half])), split(masked), NT)
-        pair = jnp.zeros((256, 256), F32)
-        for g in range(6):
-            block = slice(256 * g, 256 * g + 256)
-            pair = pair + dot3(split(field[half, block]), split(grad[half, block]), NT)
-        return both, pair
-
-    both0, pair0 = share(0, parts0)
-    both1, pair1 = share(1, parts1)
-
-    pair = pair0 + pair1
-    skip_sum = pair[:CH, :CH]
-    for i in range(1, 8):
-        block = slice(i * CH, (i + 1) * CH)
-        skip_sum = skip_sum + pair[block, block]
-    share_sum = jnp.concatenate([both0 + both1, skip_sum, jnp.zeros((CH, CH), F32)], axis=1)
+        return both, dot3(split(side_by_side(field[half])), split(side_by_side(grad[half])), NT)
+
+    both0, skip0 = share(0, parts0)
+    both1, skip1 = share(1, parts1)
+
+    share_sum = jnp.concatenate([both0 + both1, skip0 + skip1, jnp.zeros((CH, CH), F32)], axis=1)
     gsum[0] = share_sum[: CH // 2]
     gsum[1] = share_sum[CH // 2 :]
 
@@ -483,9 +475,9 @@
         store.start()
         return store
 
+    line_start(1, line_sum(0))
+
     store0 = last(0, copies4a)
-    line_start(1, line_sum(0))
-
     store1 = last(1, copies4b)
 
     scale = F32(1.0 / (BATCH * CELLS * CELLS * nx * ny))
@@ -595,7 +587,7 @@
             pltpu.VMEM((2, *half_sum), F32),
             pltpu.VMEM((2, *half_sum), F32),
             pltpu.VMEM((2, *half_sum), F32),
-            pltpu.SemaphoreType.DMA((9,)),
+            pltpu.SemaphoreType.DMA((15,)),
             pltpu.SemaphoreType.DMA((3,)),
             pltpu.SemaphoreType.DMA((4, 2, 5)),
             pltpu.SemaphoreType.DMA((4, 2, 5)),

time: 46.5 us -> 45 us (0.968)
  Pallas kernels: 45.6 us -> 44.1 us
    pallas_call x1, Pallas kernels: 42.7 us -> 41.2 us  [shards(): pl.pallas_call(functools.partial(kernel, nx, ny), out_shape=(jax.ShapeDty...]
where the time goes in v6:
time: 45 us; the launch traced here: 44.8 us
  Pallas kernels  44.1 us (98%)
  between operations  0.64 us (1%)
    pallas_call x1, Pallas kernels, shards(): pl.pallas_call(functools.partial(kernel, nx, ny), out_shape=(jax.ShapeDty...  41.2 us
    pallas_call x1, Pallas kernels, shards(): pl.pallas_call(unpack_kernel, out_shape=(jax.ShapeDtypeStruct(block, F32)...  2.94 us

profile of v6, /device:TPU:1, one launch (start us, length us, event | category | flops | bytes accessed | tf_op | source)
XLA Modules:
  0.0 44.8 jit_solution(16939980986206412878)
XLA Ops:
  0.6 41.2 %shard_map.102 = (f32[2,1536,128]{2,1,0:T(8,128)}, f32[2,16,128]{2,1,0:T(8,128)}) custom-call(f32[4,48,32,48]{3,2,1,0:T(8,128)} %bitcast.3, f32[4,48,32,48]{3,2,1,0:T(8,128)} %bitcast.4, f32[32,32]{1,0:T(8,128)} %wc_hbm.1, f32[32,32]{1,0:T(8,128)} %wd_hbm.1, f32[32,32]{1,0:T(8,128)} %ws_hbm.1, f32[512,256]{1,0:T(8,128)} %constant.4.clone.bank_hbm, ...), custom_call_target="tpu_custom_call" | custom-call | tf_op jit(solution)/shard_map/pallas_call | solution.py:554
  41.8 2.9 %shard_map.103 = (f32[4,48,32,48]{3,2,1,0:T(8,128)}, f32[32,32]{1,0:T(8,128)}, f32[32,32]{1,0:T(8,128)}, f32[32,32]{1,0:T(8,128)}) custom-call(f32[2,1536,128]{2,1,0:T(8,128)} %get-tuple-element.10.packed_hbm, f32[2,16,128]{2,1,0:T(8,128)} %get-tuple-element.11.sum_hbm), custom_call_target="tpu_custom_call" | custom-call | tf_op jit(solution)/shard_map/pallas_call | solution.py:611

commit v7 on v6

--- a/solution.py
+++ b/solution.py
@@ -220,12 +220,9 @@
     def each(axis, action):
         size, me, device = line(axis)
 
-        def step(r, carry):
+        for r in range(1, size):
             other = lax.rem(me + r, size)
             action(r, other, device(other))
-            return carry
-
-        lax.fori_loop(1, size, step, 0)
 
     for device in ((right, gy), (left, gy), (gx, up), (gx, down)):
         greet(device)
@@ -406,9 +403,13 @@
     both0, skip0 = share(0, parts0)
     both1, skip1 = share(1, parts1)
 
-    share_sum = jnp.concatenate([both0 + both1, skip0 + skip1, jnp.zeros((CH, CH), F32)], axis=1)
-    gsum[0] = share_sum[: CH // 2]
-    gsum[1] = share_sum[CH // 2 :]
+    def fold(values):
+        return jnp.concatenate([values[8 * g : 8 * g + 8] for g in range(4)], axis=1)
+
+    both = both0 + both1
+    share_sum = jnp.concatenate([fold(both[:, :CH]), fold(both[:, CH:]), fold(skip0 + skip1)], axis=0)
+    gsum[0] = share_sum[:12]
+    gsum[1] = share_sum[12:]
 
     def to_partner(phase, source, target):
         return pltpu.make_async_remote_copy(
@@ -519,10 +520,10 @@
         load.start()
     stores = []
     loads[4].wait()
+    folded = jnp.concatenate([summed[0], summed[1]], axis=0)
     for i, target in enumerate((gc_hbm, gd_hbm, gs_hbm)):
-        for part in range(2):
-            rows_here = slice(part * CH // 2, (part + 1) * CH // 2)
-            grads[i, rows_here] = summed[part, :, i * CH : (i + 1) * CH]
+        for g in range(4):
+            grads[i, 8 * g : 8 * g + 8] = folded[8 * i : 8 * i + 8, CH * g : CH * g + CH]
         store = pltpu.make_async_copy(grads.at[i], target, out_sems.at[4 + i])
         store.start()
         stores.append(store)
@@ -549,7 +550,7 @@
     weight = pltpu.VMEM((CH, CH), F32)
     small = jax.ShapeDtypeStruct((CH, CH), F32)
     peers = max(nx, ny // 2)
-    half_sum = (CH // 2, 128)
+    half_sum = (12, 128)
     bank = bank_matrix()
     packed_field, summed = pl.pallas_call(
         functools.partial(kernel, nx, ny),

time: 45 us -> 44.5 us (0.989)
  no operation moved by 1% of the time
where the time goes in v7:
time: 44.5 us; the launch traced here: 44.4 us
  Pallas kernels  43.7 us (98%)
  between operations  0.64 us (1%)
    pallas_call x1, Pallas kernels, shards(): pl.pallas_call(functools.partial(kernel, nx, ny), out_shape=(jax.ShapeDty...  40.8 us
    pallas_call x1, Pallas kernels, shards(): pl.pallas_call(unpack_kernel, out_shape=(jax.ShapeDtypeStruct(block, F32)...  2.94 us

profile of v7, /device:TPU:1, one launch (start us, length us, event | category | flops | bytes accessed | tf_op | source)
XLA Modules:
  0.0 44.4 jit_solution(3640390979603981566)
XLA Ops:
  0.6 40.8 %shard_map.102 = (f32[2,1536,128]{2,1,0:T(8,128)}, f32[2,12,128]{2,1,0:T(8,128)}) custom-call(f32[4,48,32,48]{3,2,1,0:T(8,128)} %bitcast.3, f32[4,48,32,48]{3,2,1,0:T(8,128)} %bitcast.4, f32[32,32]{1,0:T(8,128)} %wc_hbm.1, f32[32,32]{1,0:T(8,128)} %wd_hbm.1, f32[32,32]{1,0:T(8,128)} %ws_hbm.1, f32[512,256]{1,0:T(8,128)} %constant.4.clone.bank_hbm, ...), custom_call_target="tpu_custom_call" | custom-call | tf_op jit(solution)/shard_map/pallas_call | solution.py:555
  41.4 2.9 %shard_map.103 = (f32[4,48,32,48]{3,2,1,0:T(8,128)}, f32[32,32]{1,0:T(8,128)}, f32[32,32]{1,0:T(8,128)}, f32[32,32]{1,0:T(8,128)}) custom-call(f32[2,1536,128]{2,1,0:T(8,128)} %get-tuple-element.10.packed_hbm, f32[2,12,128]{2,1,0:T(8,128)} %get-tuple-element.11.sum_hbm), custom_call_target="tpu_custom_call" | custom-call | tf_op jit(solution)/shard_map/pallas_call | solution.py:612

commit v8 on v7

--- a/solution.py
+++ b/solution.py
@@ -19,6 +19,9 @@
     -0.010597401784997278,
 ]
 HIGH_TAPS = [(-1) ** offset * LOW_TAPS[7 - offset] for offset in range(8)]
+
+UNIT_LOW = [tap / LOW_TAPS[1] for tap in LOW_TAPS]
+UNIT_HIGH = [tap / LOW_TAPS[1] for tap in HIGH_TAPS]
 
 F32 = jnp.float32
 BF16 = jnp.bfloat16
@@ -71,7 +74,7 @@
                         for k in range(COARSE):
                             lane = ((xband * 2 + yband) * COARSE + k) * 2 + b
                             result[group, xband, b, :CELLS, part, group, lane] = line[yband, part * COARSE + k]
-    return result.reshape(512, 256).astype(np.float32)
+    return (LOW_TAPS[1] ** 3 * result).reshape(512, 256).astype(np.float32)
 
 
 def split(values):
@@ -89,12 +92,16 @@
 NT = ((1,), (1,))
 
 
+def times(values, tap):
+    return values if tap == 1.0 else values * F32(tap)
+
+
 class Analysis:
     def __init__(self, load):
         self.load = load
         self.memo = {}
 
-    def get(self, level, k, taps=LOW_TAPS, band=0):
+    def get(self, level, k, taps=UNIT_LOW, band=0):
         if level == 0:
             if (0, k) not in self.memo:
                 self.memo[0, k] = self.load(k)
@@ -105,7 +112,7 @@
             total = None
             for j in range(8):
                 if low <= 2 * k + j <= high:
-                    term = self.get(level - 1, 2 * k + j) * F32(taps[j])
+                    term = times(self.get(level - 1, 2 * k + j), taps[j])
                     total = term if total is None else total + term
             self.memo[key] = total
         return self.memo[key]
@@ -130,9 +137,9 @@
                 j = i - 2 * k
                 if 0 <= j < 8:
                     if level == 2:
-                        term = self.top(0, k) * F32(LOW_TAPS[j]) + self.top(1, k) * F32(HIGH_TAPS[j])
+                        term = times(self.top(0, k), UNIT_LOW[j]) + times(self.top(1, k), UNIT_HIGH[j])
                     else:
-                        term = self.get(level + 1, k) * F32(LOW_TAPS[j])
+                        term = times(self.get(level + 1, k), UNIT_LOW[j])
                     total = term if total is None else total + term
             self.memo[key] = total
         return self.memo[key]
@@ -153,7 +160,7 @@
     for k in range(-COARSE, COARSE):
         part, group, row = (k + COARSE) // 6, (k + COARSE) % 6 // 3, (k + COARSE) % 3
         start = (part * 3 + row) * CH
-        for band, taps in enumerate((LOW_TAPS, HIGH_TAPS)):
+        for band, taps in enumerate((UNIT_LOW, UNIT_HIGH)):
             lanes = group * 256 + band * 128
             lines[pl.ds(pl.multiple_of(start + rows, 8), 8), lanes : lanes + 128] = walk.get(3, k, taps, band)
 

time: 44.5 us -> 44.3 us (level)
  no operation moved by 1% of the time
where the time goes in v8:
time: 44.3 us; the launch traced here: 44.2 us
  Pallas kernels  43.6 us (98%)
  between operations  0.64 us (1%)
    pallas_call x1, Pallas kernels, shards(): pl.pallas_call(functools.partial(kernel, nx, ny), out_shape=(jax.ShapeDty...  40.7 us
    pallas_call x1, Pallas kernels, shards(): pl.pallas_call(unpack_kernel, out_shape=(jax.ShapeDtypeStruct(block, F32)...  2.94 us

profile of v8, /device:TPU:1, one launch (start us, length us, event | category | flops | bytes accessed | tf_op | source)
XLA Modules:
  0.0 44.2 jit_solution(2913947811858187742)
XLA Ops:
  0.6 40.7 %shard_map.102 = (f32[2,1536,128]{2,1,0:T(8,128)}, f32[2,12,128]{2,1,0:T(8,128)}) custom-call(f32[4,48,32,48]{3,2,1,0:T(8,128)} %bitcast.3, f32[4,48,32,48]{3,2,1,0:T(8,128)} %bitcast.4, f32[32,32]{1,0:T(8,128)} %wc_hbm.1, f32[32,32]{1,0:T(8,128)} %wd_hbm.1, f32[32,32]{1,0:T(8,128)} %ws_hbm.1, f32[512,256]{1,0:T(8,128)} %constant.4.clone.bank_hbm, ...), custom_call_target="tpu_custom_call" | custom-call | tf_op jit(solution)/shard_map/pallas_call | solution.py:562
  41.3 2.9 %shard_map.103 = (f32[4,48,32,48]{3,2,1,0:T(8,128)}, f32[32,32]{1,0:T(8,128)}, f32[32,32]{1,0:T(8,128)}, f32[32,32]{1,0:T(8,128)}) custom-call(f32[2,1536,128]{2,1,0:T(8,128)} %get-tuple-element.10.packed_hbm, f32[2,12,128]{2,1,0:T(8,128)} %get-tuple-element.11.sum_hbm), custom_call_target="tpu_custom_call" | custom-call | tf_op jit(solution)/shard_map/pallas_call | solution.py:619
